TPU v7x, 256 devices: a whole 4x4x8 slice. The times are simulated.
256 devices in a mesh: tok: 64 (over z, x, core), hv: 4 (over y).
Axes of the slice: x: 4, y: 4, z: 8, core: 2. Of those that a mesh axis runs over, the one named last changes fastest.
Arguments:
- tokens: bfloat16 [16384, 2048], P(('tok', 'hv')), may hold values from -6 to 6
- prompt_lengths: int32 [33], replicated, may hold values from 1 to 10922, 16384 in all
- query_weight: bfloat16 [2048, 1024], P(None, 'hv'), may hold values from -0.125 to 0.125
- key_weight: bfloat16 [2048, 1024], P(None, 'hv'), may hold values from -0.125 to 0.125
- value_weight: bfloat16 [2048, 2048], P(None, 'hv'), may hold values from -0.125 to 0.125
- query_conv: bfloat16 [4, 1024], P(None, 'hv'), may hold values from -3 to 3
- key_conv: bfloat16 [4, 1024], P(None, 'hv'), may hold values from -3 to 3
- value_conv: bfloat16 [4, 2048], P(None, 'hv'), may hold values from -3 to 3
- decay_down: bfloat16 [2048, 16], replicated, may hold values from -0.125 to 0.125
- decay_up: bfloat16 [16, 1024], P(None, 'hv'), may hold values from -3 to 3
- decay_bias: float32 [1024], P('hv')
- gate_weight: bfloat16 [2048, 2048], P(None, 'hv'), may hold values from -0.125 to 0.125
- norm_gain: float32 [512], replicated, may hold values from 0.1 to 1.9
- out_weight: bfloat16 [2048, 2048], P('hv'), may hold values from -0.125 to 0.125
Outputs:
- mixed: bfloat16 [16384, 2048], P(('tok', 'hv'))
- segment_states: float32 [64, 4, 256, 512], P('tok', 'hv')
- conv_edges: bfloat16 [64, 3, 4, 1024], P('tok', None, 'hv')
Inputs may be any that keep to these rules, and one draw needn't show every extreme that they name: `prompt_lengths`: the rows of 33 prompts that fill all 16384 packed rows; exactly one prompt has 10922 rows.
All inputs are finite; a program needn't handle non-finite values.
Results may differ from a plain program's by a relative error of at most 0.022.
Values may be sent and summed in bfloat16 or wider, within the bound.
A program may use at most 128 MiB of HBM per device.

v0:
```python
import jax
import jax.numpy as jnp
from jax import lax
from jax.sharding import PartitionSpec as P

SPAN = 64


HIGHEST_PRECISION = lax.Precision.HIGHEST


def shifted(value, axis, steps):
    count = lax.axis_size(axis)
    initial, last = (max(0, -steps), min(count, count - steps))
    return lax.ppermute(value, axis, [(source, source + steps) for source in range(initial, last)])


def carried_in(part, axis, combine, identity):
    place = lax.axis_index(axis)
    gathered = jax.tree.map(lambda a: lax.all_gather(a, axis), part)
    state = jax.tree.map(lambda a, e: jnp.zeros_like(a) + jnp.asarray(e, a.dtype), part, identity)

    def one(lap, state):
        return combine(
            state, jax.tree.map(lambda a: lax.dynamic_index_in_dim(a, lap, 0, False), gathered)
        )

    return lax.fori_loop(0, place, one, state)


def prompt_marks(positions, offsets):
    before = offsets[None, :] <= positions[:, None]
    prompt_first = jnp.max(jnp.where(before, offsets[None, :], 0), axis=1)
    return (prompt_first, (prompt_first == positions).astype(jnp.float32))


def short_conv(raw_rows, before_rows, weight, positions, prompt_first):
    tap_count = weight.shape[0]
    extended = jnp.concatenate([before_rows, raw_rows], axis=0)
    summed = jnp.zeros(raw_rows.shape, jnp.float32)
    for tap_index in range(tap_count):
        lag_rows = tap_count - 1 - tap_index
        inside_prompt = (positions - lag_rows >= prompt_first).astype(jnp.float32)
        window = lax.slice_in_dim(extended, tap_index, tap_index + raw_rows.shape[0], axis=0)
        summed = (
            summed
            + weight[tap_index].astype(jnp.float32)[None, :]
            * window.astype(jnp.float32)
            * inside_prompt[:, None]
        )
    return jax.nn.silu(summed).astype(jnp.bfloat16)


def span_parts(head_keys, head_values, decays, starts):
    cumulative = jnp.cumsum(decays, axis=0)
    groups = jnp.cumsum(starts)
    intact = (groups == 0.0).astype(jnp.float32)
    final_log = cumulative[-1]
    in_tail = (groups == groups[-1]).astype(jnp.float32)
    weighted = (
        head_keys.astype(jnp.float32) * jnp.exp(final_log[None, :] - cumulative) * in_tail[:, None]
    ).astype(jnp.bfloat16)
    update = lax.dot_general(
        weighted, head_values, (((0,), (0,)), ((), ())), preferred_element_type=jnp.float32
    )
    step_decay = jnp.exp(final_log) * intact[-1]
    return (cumulative, groups, intact, update, step_decay)


def state_step(carried, pieces):
    memory, product = carried
    head_keys, head_values, decays, starts = pieces
    _, _, _, update, step_decay = span_parts(head_keys, head_values, decays, starts)
    return ((step_decay[:, None] * memory + update, product * step_decay), None)


def span_step(carried, pieces):
    memory, product = carried
    queries, head_keys, head_values, decays, starts = pieces
    cumulative, groups, intact, update, step_decay = span_parts(
        head_keys, head_values, decays, starts
    )
    index_rows = jnp.arange(queries.shape[0])
    allowed = (groups[:, None] == groups[None, :]) & (index_rows[:, None] >= index_rows[None, :])
    lifted = queries.astype(jnp.float32) * jnp.exp(cumulative)
    lowered = (head_keys.astype(jnp.float32) * jnp.exp(-cumulative)).astype(jnp.bfloat16)
    raw_scores = lax.dot_general(
        lifted.astype(jnp.bfloat16),
        lowered,
        (((1,), (1,)), ((), ())),
        preferred_element_type=jnp.float32,
    )
    scores = jnp.where(allowed, raw_scores, 0.0).astype(jnp.bfloat16)
    inside = jnp.dot(scores, head_values, preferred_element_type=jnp.float32)
    outside = jnp.dot(lifted * intact[:, None], memory, precision=HIGHEST_PRECISION)
    reaches = product[None, :] * jnp.exp(cumulative) * intact[:, None]
    return (
        (step_decay[:, None] * memory + update, product * step_decay),
        (inside + outside, reaches),
    )


def blocked(array_in):
    return array_in.reshape((array_in.shape[0] // SPAN, SPAN) + array_in.shape[1:])


def sweep(queries, head_keys, head_values, decays, starts, memory):
    initial = (memory, jnp.ones((decays.shape[1],), jnp.float32))
    (closing, product), (outputs, reaches) = lax.scan(
        span_step,
        initial,
        (
            blocked(queries),
            blocked(head_keys),
            blocked(head_values),
            blocked(decays),
            blocked(starts),
        ),
    )
    row_count = queries.shape[0]
    return (
        outputs.reshape((row_count, head_values.shape[1])),
        reaches.reshape((row_count, decays.shape[1])),
        closing,
        product,
    )


def combine(earlier, following):
    return (earlier[0] * following[0], following[0][:, None] * earlier[1] + following[1])


def shards(
    tokens,
    prompt_lengths,
    query_weight,
    key_weight,
    value_weight,
    query_conv,
    key_conv,
    value_conv,
    decay_down,
    decay_up,
    decay_bias,
    gate_weight,
    norm_gain,
    out_weight,
):
    gathered = lax.all_gather(tokens, "hv", axis=0, tiled=True)

    def project(weight):
        return jnp.dot(gathered, weight, preferred_element_type=jnp.float32).astype(jnp.bfloat16)

    raw_query = project(query_weight)
    raw_key = project(key_weight)
    raw_value = project(value_weight)
    gate_values = project(gate_weight)
    low_rank = project(decay_down)
    row_count = raw_query.shape[0]
    key_width = raw_query.shape[1]
    value_width = raw_value.shape[1]
    positions = lax.axis_index("tok") * row_count + jnp.arange(row_count, dtype=jnp.int32)
    offsets = jnp.cumsum(prompt_lengths) - prompt_lengths
    prompt_first, starts = prompt_marks(positions, offsets)
    rim_rows = query_conv.shape[0] - 1
    joined = jnp.concatenate([raw_query, raw_key, raw_value], axis=1)
    before_rows = shifted(joined[row_count - rim_rows :], "tok", 1)
    conv_query = short_conv(
        raw_query, before_rows[:, :key_width], query_conv, positions, prompt_first
    )
    conv_key = short_conv(
        raw_key, before_rows[:, key_width : 2 * key_width], key_conv, positions, prompt_first
    )
    conv_value = short_conv(
        raw_value, before_rows[:, 2 * key_width :], value_conv, positions, prompt_first
    )
    decays = (
        jax.nn.log_sigmoid(
            jnp.dot(low_rank, decay_up, preferred_element_type=jnp.float32) + decay_bias
        )
        / 16.0
    )
    empty_memory = jnp.zeros((key_width, value_width), jnp.float32)
    ones_decay = jnp.ones((key_width,), jnp.float32)
    (local_memory, local_decay), _ = lax.scan(
        state_step,
        (empty_memory, ones_decay),
        (blocked(conv_key), blocked(conv_value), blocked(decays), blocked(starts)),
    )
    entering_decay, entering = carried_in(
        (local_decay, local_memory), "tok", combine, (ones_decay, empty_memory)
    )
    heads_out, _, closing, _ = sweep(conv_query, conv_key, conv_value, decays, starts, entering)
    gate_float = gate_values.astype(jnp.float32)
    rescale = lax.rsqrt(jnp.mean(heads_out * heads_out, axis=1, keepdims=True) + 1e-05)
    gated_out = (
        heads_out * rescale * norm_gain[None, :] * gate_float * jax.nn.sigmoid(gate_float)
    ).astype(jnp.bfloat16)
    mixed = lax.psum_scatter(
        jnp.dot(gated_out, out_weight, preferred_element_type=jnp.float32).astype(jnp.bfloat16),
        "hv",
        scatter_dimension=0,
        tiled=True,
    )
    segment_states = closing[None, None]
    in_prompt = positions[row_count - rim_rows :] >= prompt_first[row_count - 1]
    tail_rows = joined[row_count - rim_rows :]
    conv_edges = jnp.where(in_prompt[:, None], tail_rows, jnp.zeros_like(tail_rows))
    conv_edges = conv_edges.reshape((1, rim_rows, 1, joined.shape[1]))
    return (mixed, segment_states, conv_edges)


def solution(mesh):
    in_specs = (
        P(("tok", "hv"), None),
        P(),
        P(None, "hv"),
        P(None, "hv"),
        P(None, "hv"),
        P(None, "hv"),
        P(None, "hv"),
        P(None, "hv"),
        P(),
        P(None, "hv"),
        P("hv"),
        P(None, "hv"),
        P(),
        P("hv", None),
    )
    out_specs = (P(("tok", "hv"), None), P("tok", "hv", None, None), P("tok", None, "hv", None))
    return jax.shard_map(shards, mesh=mesh, in_specs=in_specs, out_specs=out_specs, check_vma=False)
```

profile of v0, /device:TPU:1, one launch (start us, length us, event | category | flops | bytes accessed | tf_op | source)
XLA Modules:
  0.0 348.0 jit_solution(8499154411287329581)
XLA Ops:
  7.2 0.7 all-gather.6.cloned.1.call-update
  8.0 0.8 copy.28
  8.9 0.7 sub.48
  10.3 0.7 slice_compare_fusion
  11.6 1.4 slice_convert_fusion.11
  13.0 0.8 slice_convert_fusion.3
  13.8 25.5 %all-gather.6.cloned.1.call-done = bf16[256,2048]{1,0:T(8,128)(2,1)} async-done(((bf16[64,2048]{1,0:T(8,128)(2,1)}), bf16[256,2048]{1,0:T(8,128)(2,1)}) %all-gather.6.cloned.1.call-update) | async-done | bytes 1048592 | tf_op jit(solution)/shard_map/all_gather | solution.py:149
  39.3 2.8 convolution_convert_fusion.2
  43.0 0.7 select_bitcast_fusion
  43.7 4.5 %collective-permute-start = (bf16[3,1024]{1,0:T(4,128)(2,1)S(1)}, bf16[3,1024]{1,0:T(4,128)(2,1)S(1)}, u32[]{:S(2)}, u32[]{:S(2)}) collective-permute-start(bf16[3,1024]{1,0:T(4,128)(2,1)S(1)} %get-tuple-element.200), channel_id=1, source_target_pairs={{0,4},{4,8},{8,12},{12,16},{16,20},{20,24},{24,28},{28,32},{32,36}... | collective-permute-start | bytes 18440 | tf_op jit(solution)/shard_map/ppermute | solution.py:15
  48.3 2.0 fusion.69
  50.4 2.0 multiply_convert_fusion
  52.9 0.9 multiply_convert_fusion.2
  53.9 13.0 %while.39 = (s32[]{:T(128)}, f32[256,512]{1,0:T(8,128)S(1)}, f32[256]{0:T(256)S(1)}, f32[4,64,256]{2,1,0:T(8,128)S(1)}, f32[4,64]{1,0:T(4,128)}, /*index=5*/bf16...) while((s32[]{:T(128)}, f32[256,512]{1,0:T(8,128)S(1)}, ...), condition=%wide.region_5.6_spmd.clone, body=%wide.region_2.5_spmd.clone.sunk | while | flops 18289476 | bytes 1486494 | solution.py:185
  54.0 0.6 fusion.115
  56.0 0.8 convert_reduce_fusion.2
  59.3 0.8 convert_reduce_fusion.2
  60.5 0.6 fusion.115
  62.5 0.8 convert_reduce_fusion.2
  65.8 0.8 convert_reduce_fusion.2
  66.9 0.8 copy-done.2
  67.8 0.8 slice_convert_fusion.7
  68.6 45.6 %all-gather.2 = f32[64,1,256]{2,1,0:T(1,128)S(1)} all-gather(f32[1,1,256]{2,1,0:T(1,128)S(1)} %bitcast.205), channel_id=2, replica_groups=mesh['tok'=64,'hv'=4] {'tok'}, dimensions={0}, use_global_device_ids=true | all-gather | bytes 66560 | tf_op jit(solution)/shard_map/all_gather | solution.py:20
  114.2 1.7 multiply_convert_fusion.1
  115.9 95.1 %all-gather.8.cloned.1.call-done = f32[16384,512]{1,0:T(8,128)} async-done(((f32[256,512]{1,0:T(8,128)}), f32[16384,512]{1,0:T(8,128)}) %all-gather.8.cloned.1.call-update) | async-done | bytes 33554448 | tf_op jit(solution)/shard_map/all_gather | solution.py:20
  211.0 1.2 while.37
  211.1 1.2 bitcast_add_fusion.2
  212.3 27.2 %while.38 = (s32[]{:T(128)}, f32[256,512]{1,0:T(8,128)S(1)}, f32[4,64,512]{2,1,0:T(8,128)}, f32[4,64,256]{2,1,0:T(8,128)S(1)}, f32[4,64]{1,0:T(4,128)}, /*index=...) while((s32[]{:T(128)}, f32[256,512]{1,0:T(8,128)S(1)}, ...), condition=%wide.region_11.12_spmd, body=%wide.region_8.11_spmd.sunk | while | flops 125329856 | bytes 2767001 | solution.py:109
  213.4 1.0 fusion.111
  214.9 0.6 compare_convert_fusion.7
  215.6 1.9 fusion.112
  218.0 0.6 exponential_multiply_fusion.4
  220.2 1.0 fusion.111
  221.7 0.6 compare_convert_fusion.7
  222.4 1.9 fusion.112
  224.8 0.6 exponential_multiply_fusion.4
  226.9 1.0 fusion.111
  228.5 0.6 compare_convert_fusion.7
  229.2 1.9 fusion.112
  231.7 0.6 exponential_multiply_fusion.4
  233.8 1.0 fusion.111
  235.3 0.6 compare_convert_fusion.7
  236.0 1.9 fusion.112
  238.4 0.6 exponential_multiply_fusion.4
  239.5 1.3 multiply_reduce_fusion
  241.0 2.8 fusion.65
  243.8 1.7 convolution_convert_fusion
  245.5 96.0 %reduce-scatter.2.cloned.1.call-done = bf16[64,2048]{1,0:T(8,128)(2,1)} async-done(((bf16[256,2048]{1,0:T(8,128)(2,1)}), bf16[64,2048]{1,0:T(8,128)(2,1)}) %reduce-scatter.2.cloned.1.call-update) | async-done | bytes 262160 | tf_op jit(solution)/shard_map/reduce_scatter | solution.py:199
  (125 shorter events, 19.4 us)
Async XLA Ops:
  7.2 236.6 %copy-start = (bf16[512,2048]{1,0:T(8,128)(2,1)S(1)}, bf16[512,2048]{1,0:T(8,128)(2,1)}, u32[]{:S(2)}) copy-start(bf16[512,2048]{1,0:T(8,128)(2,1)} %param.33) | copy-start | bytes 6291460
  7.2 32.1 %all-gather.6.cloned.1.call-start = ((), (), s32[]{:S(2)}) async-start(), calls=%async_computation.1 | async-start | bytes 1310720 | tf_op jit(solution)/shard_map/all_gather | solution.py:149
  7.9 203.1 %all-gather.8.cloned.1.call-start = ((), (), s32[]{:S(2)}) async-start(), calls=%async_computation.3 | async-start | bytes 34078720 | tf_op jit(solution)/shard_map/all_gather | solution.py:20
  11.6 38.8 %copy-start.8 = (f32[256]{0:T(256)}, f32[256]{0:T(256)S(1)}, u32[]{:S(2)}) copy-start(f32[256]{0:T(256)S(1)} %get-tuple-element.220) | copy-start | bytes 3076
  11.6 41.3 %copy-start.7 = (f32[256]{0:T(256)}, f32[256]{0:T(256)S(1)}, u32[]{:S(2)}) copy-start(f32[256]{0:T(256)S(1)} %get-tuple-element.219) | copy-start | bytes 3076
  39.3 2.8 copy-start.3
  39.3 2.8 copy-start.5
  39.3 3.3 copy-start.6
  42.1 0.9 copy-start.4
  42.1 6.2 %copy-start.9 = (bf16[2048,16]{0,1:T(8,128)(2,1)S(1)}, bf16[2048,16]{0,1:T(8,128)(2,1)}, u32[]{:S(2)}) copy-start(bf16[2048,16]{0,1:T(8,128)(2,1)} %param.28) | copy-start | bytes 196612
  42.1 6.2 %copy-start.10 = (bf16[16,256]{1,0:T(8,128)(2,1)S(1)}, bf16[16,256]{1,0:T(8,128)(2,1)}, u32[]{:S(2)}) copy-start(bf16[16,256]{1,0:T(8,128)(2,1)} %param.29) | copy-start | bytes 24580
  42.1 6.2 %copy-start.12 = (f32[256]{0:T(256)S(1)}, f32[256]{0:T(256)}, u32[]{:S(2)}) copy-start(f32[256]{0:T(256)} %param.30) | copy-start | bytes 3076
  43.7 6.6 %collective-permute-start = (bf16[3,1024]{1,0:T(4,128)(2,1)S(1)}, bf16[3,1024]{1,0:T(4,128)(2,1)S(1)}, u32[]{:S(2)}, u32[]{:S(2)}) collective-permute-start(bf16[3,1024]{1,0:T(4,128)(2,1)S(1)} %get-tuple-element.200), channel_id=1, source_target_pairs={{0,4},{4,8},{8,12},{12,16},{16,20},{20,24},{24,28},{28,32},{32,36}... | collective-permute-start | bytes 18440 | tf_op jit(solution)/shard_map/ppermute | solution.py:15
  66.9 0.8 copy-start.2
  67.7 273.7 %reduce-scatter.2.cloned.1.call-start = ((), (), s32[]{:S(2)}) async-start(), calls=%async_computation.2 | async-start | bytes 1310720 | tf_op jit(solution)/shard_map/reduce_scatter | solution.py:199
  212.3 28.7 %copy-start.11 = (f32[512]{0:T(512)S(1)}, f32[512]{0:T(512)}, u32[]{:S(2)}) copy-start(f32[512]{0:T(512)} %param.32) | copy-start | bytes 6148
  239.5 4.2 %copy-start.1 = (f32[256,512]{1,0:T(8,128)}, f32[256,512]{1,0:T(8,128)S(1)}, u32[]{:S(2)}) copy-start(f32[256,512]{1,0:T(8,128)S(1)} %get-tuple-element.132) | copy-start | bytes 1572868
Sparse Core Ops, SparseCore 0:
  9.8 29.4 all-gather.5
  67.8 143.0 all-gather.7
  245.6 95.8 reduce-scatter.1
where the time goes:
time: 353 us; the launch traced here: 348 us
  waiting for transfers between devices  217 us (61%)
  blocking collectives  45.6 us (13%)
  matrix products  24.7 us (7%)
  other arithmetic  23.3 us (7%)
  local copies, waits for them, and re-layouts  15.4 us (4%)
  between operations  14 us (4%)
  starting transfers between devices  4.67 us (1%)
    reduce_scatter x1, waiting for transfers between devices, shards(): lax.psum_scatter(jnp.dot(gated_out, out_weight, preferred_element_type=jn...  96 us
    all_gather x1, waiting for transfers between devices, carried_in(): gathered = jax.tree.map(lambda a: lax.all_gather(a, axis), part)  95.1 us
    all_gather x1, blocking collectives, carried_in(): gathered = jax.tree.map(lambda a: lax.all_gather(a, axis), part)  45.6 us
    all_gather x1, waiting for transfers between devices, shards(): gathered = lax.all_gather(tokens, 'hv', axis=0, tiled=True)  25.5 us
    dot_general x4, matrix products, span_step(): jnp.dot(lifted * intact[:, None], memory, precision=HIGHEST_PRECISION)  7.52 us
  transfers between devices with their start and end apart: 4, of which 3 were waited for; matrix products, arithmetic and copies ran while one was open for 3% of the time, Pallas kernels for 0%

commit v1 on v0

v1 whole, which is shorter than its diff:
```python
import functools

import jax
import jax.numpy as jnp
from jax import lax
from jax.experimental import pallas as pl
from jax.experimental.pallas import tpu as pltpu
from jax.sharding import PartitionSpec as P

MESH = pl.DeviceIdType.MESH
F32 = jnp.float32
BF16 = jnp.bfloat16
HIGHEST = lax.Precision.HIGHEST

HV = 4
GROUP = 8
PLANES = 8
ROWS = 64
SEG = 256
D = 2048
DK = 256
DV = 512
QKV = 2 * DK + DV
WIDE = QKV + DV
CHUNK = 512
PIECE = DK // GROUP


def dot(a, b):
    return jnp.dot(a, b, preferred_element_type=F32)


def dot_nt(a, b):
    return lax.dot_general(a, b, (((1,), (1,)), ((), ())), preferred_element_type=F32)


def dot_tn(a, b):
    return lax.dot_general(a, b, (((0,), (0,)), ((), ())), preferred_element_type=F32)


def across(a, copies):
    return jnp.concatenate([a] * copies, axis=1)


def kernel(
    tokens,
    lengths,
    wq,
    wk,
    wv,
    cq,
    ck,
    cv,
    wdown,
    wup,
    bias,
    wg,
    gain,
    wout,
    mixed,
    states,
    edges,
    xt,
    wall,
    wlow,
    wo,
    taps_q,
    taps_k,
    taps_v,
    up,
    bias_v,
    gain_v,
    lens,
    acc,
    accl,
    ext,
    halo,
    pf_col,
    pf_row,
    keep,
    cum,
    convk,
    convv,
    local,
    lifted,
    inner,
    gg,
    dsend,
    dgat,
    gsend,
    ggat,
    dmat,
    dt,
    l1s,
    l1r,
    p1,
    t2s,
    t2r,
    q2s,
    q2r,
    e1s,
    er,
    rs_s,
    relay,
    fl,
    fr,
    w_sem,
    loc_sem,
    tk_send,
    tk_recv,
    halo_sem,
    d_send,
    d_recv,
    g_send,
    g_recv,
    l1_send,
    l1_recv,
    t2_send,
    t2_recv,
    q2_send,
    q2_recv,
    e1_send,
    e1_recv,
    rs_send,
    relay_recv,
    fl_recv,
    fr_recv,
):
    tok = lax.axis_index("tok")
    y = lax.axis_index("hv")
    n_tok = GROUP * PLANES
    z = lax.div(tok, GROUP)
    g = lax.rem(tok, GROUP)
    right = lax.rem(y + 1, HV)
    left = lax.rem(y + HV - 1, HV)
    opp = lax.rem(y + 2, HV)
    after = lax.rem(tok + 1, n_tok)
    before = lax.rem(tok + n_tok - 1, n_tok)

    def remote(src, dst, ss, rs, to_tok, to_hv):
        return pltpu.make_async_remote_copy(
            src_ref=src, dst_ref=dst, send_sem=ss, recv_sem=rs, device_id=(to_tok, to_hv), device_id_type=MESH
        )

    def mate(k):
        return lax.rem(g + k, GROUP)

    def peer(k):
        return lax.rem(z + k, PLANES)

    own = pltpu.make_async_copy(tokens, xt.at[y], loc_sem.at[0])
    own.start()

    def weight_copies(c):
        rows = pl.ds(c * CHUNK, CHUNK)
        return [
            pltpu.make_async_copy(wq.at[rows], wall.at[rows, 0:DK], w_sem.at[c, 0]),
            pltpu.make_async_copy(wk.at[rows], wall.at[rows, DK : 2 * DK], w_sem.at[c, 1]),
            pltpu.make_async_copy(wv.at[rows], wall.at[rows, 2 * DK : QKV], w_sem.at[c, 2]),
            pltpu.make_async_copy(wg.at[rows], wall.at[rows, QKV:WIDE], w_sem.at[c, 3]),
        ]

    small = [
        pltpu.make_async_copy(src, dst, loc_sem.at[1 + i])
        for i, (src, dst) in enumerate(
            [
                (lengths, lens),
                (wdown, wlow),
                (wup, up),
                (bias, bias_v),
                (gain, gain_v),
                (cq, taps_q),
                (ck, taps_k),
                (cv, taps_v),
                (wout, wo),
            ]
        )
    ]

    barrier = pltpu.get_barrier_semaphore()
    pl.semaphore_signal(barrier, inc=1, device_id=(tok, right), device_id_type=MESH)
    pl.semaphore_signal(barrier, inc=1, device_id=(tok, left), device_id_type=MESH)
    pl.semaphore_signal(barrier, inc=1, device_id=(after, y), device_id_type=MESH)
    pl.semaphore_signal(barrier, inc=1, device_id=(before, y), device_id_type=MESH)
    for k in range(1, GROUP):
        pl.semaphore_signal(barrier, inc=1, device_id=(z * GROUP + mate(k), y), device_id_type=MESH)
    for k in range(1, PLANES):
        pl.semaphore_signal(barrier, inc=1, device_id=(peer(k) * GROUP + g, y), device_id_type=MESH)
    for copy in small[:2]:
        copy.start()
    for c in range(D // CHUNK):
        for copy in weight_copies(c):
            copy.start()
    for copy in small[2:]:
        copy.start()
    pl.semaphore_wait(barrier, 4 + GROUP - 1 + PLANES - 1)

    def cols(c):
        return pl.ds(pl.multiple_of(c * CHUNK, CHUNK), CHUNK)

    def own_to_right(s):
        return remote(
            tokens.at[:, cols(s)], xt.at[y, :, cols(s)], tk_send.at[0, s], tk_recv.at[0, s], tok, right
        )

    def own_to_left(s):
        c = lax.rem(s + 2, 4)
        return remote(
            tokens.at[:, cols(c)], xt.at[y, :, cols(c)], tk_send.at[1, s], tk_recv.at[1, s], tok, left
        )

    def from_left(s):
        part = xt.at[left, :, cols(s)]
        return remote(part, part, tk_send.at[0, s], tk_recv.at[0, s], tok, right)

    def from_right(s):
        part = xt.at[right, :, cols(lax.rem(s + 2, 4))]
        return remote(part, part, tk_send.at[1, s], tk_recv.at[1, s], tok, left)

    def on_to_right(f):
        part = xt.at[left, :, cols(f)]
        return remote(part, part, tk_send.at[0, 4 + f], tk_recv.at[0, 4 + f], tok, right)

    def on_to_left(f):
        part = xt.at[right, :, cols(f + 2)]
        return remote(part, part, tk_send.at[1, 4 + f], tk_recv.at[1, 4 + f], tok, left)

    def far_from_left(f):
        part = xt.at[opp, :, cols(f)]
        return remote(part, part, tk_send.at[0, 4 + f], tk_recv.at[0, 4 + f], tok, right)

    def far_from_right(f):
        part = xt.at[opp, :, cols(f + 2)]
        return remote(part, part, tk_send.at[1, 4 + f], tk_recv.at[1, 4 + f], tok, left)

    for s in range(4):
        own_to_right(s).start()
        own_to_left(s).start()

    acc[...] = jnp.zeros_like(acc)
    accl[...] = jnp.zeros_like(accl)

    for copy in small[:2]:
        copy.wait()
    first = tok * SEG
    pos_col = first + lax.broadcasted_iota(jnp.int32, (SEG, 128), 0)
    pos_row = first + lax.broadcasted_iota(jnp.int32, (8, SEG), 1)

    def mark(j, carried):
        offset, col, row = carried
        col = jnp.where(offset <= pos_col, offset, col)
        row = jnp.where(offset <= pos_row, offset, row)
        return offset + lens[j], col, row

    _, col, row = lax.fori_loop(
        0,
        lens.shape[0],
        mark,
        (jnp.int32(0), jnp.zeros((SEG, 128), jnp.int32), jnp.zeros((8, SEG), jnp.int32)),
    )
    pf_col[...] = col
    pf_row[...] = row
    for lag in range(1, 4):
        keep[lag - 1] = jnp.where(pos_col - lag >= col, 1.0, 0.0)

    def gemm(block, c):
        x = xt[block, :, cols(c)]
        for n in range(0, WIDE, CHUNK):
            acc[block, :, n : n + CHUNK] += dot(x, wall[cols(c), n : n + CHUNK])
        accl[block] += dot(x, wlow[cols(c), :])

    own.wait()

    def own_step(c, _):
        for copy in weight_copies(c):
            copy.wait()
        gemm(y, c)
        return 0

    lax.fori_loop(0, 4, own_step, 0)

    def near_step(s, _):
        from_left(s).wait_recv()
        on_to_right(s).start()
        from_right(s).wait_recv()
        on_to_left(s).start()
        gemm(left, s)
        gemm(right, s + 2)
        return 0

    lax.fori_loop(0, 2, near_step, 0)

    def near_step2(s, _):
        from_left(s).wait_recv()
        gemm(left, s)
        from_right(s).wait_recv()
        gemm(right, s - 2)
        return 0

    lax.fori_loop(2, 4, near_step2, 0)

    def far_step(f, _):
        far_from_left(f).wait_recv()
        gemm(opp, f)
        far_from_right(f).wait_recv()
        gemm(opp, f + 2)
        return 0

    lax.fori_loop(0, 2, far_step, 0)

    for b in (3, 0, 1, 2):
        ext[8 + b * ROWS : 8 + (b + 1) * ROWS, :] = acc[b, :, 0:QKV].astype(BF16).astype(F32)
        if b == 3:
            halo_copy = remote(
                ext.at[SEG : SEG + 8], halo, halo_sem.at[0], halo_sem.at[1], after, y
            )
            halo_copy.start()

    for copy in small[2:]:
        copy.wait()

    row_i = lax.broadcasted_iota(jnp.int32, (SEG, SEG), 0)
    col_i = lax.broadcasted_iota(jnp.int32, (SEG, SEG), 1)
    tri = jnp.where(row_i >= col_i, 1.0, 0.0).astype(F32)
    low = accl[...].reshape(SEG, accl.shape[2]).astype(BF16)
    v = dot(low, up[...]) + bias_v[...]
    decays = (jnp.minimum(v, 0.0) - jnp.log1p(jnp.exp(-jnp.abs(v)))) * (1.0 / 16.0)
    cum[...] = jnp.dot(tri, decays, precision=HIGHEST, preferred_element_type=F32)
    c_last = cum[SEG - 1 : SEG, :]
    pf_last = pf_col[SEG - 1 : SEG, :]
    whole = jnp.where(pf_last < first, 1.0, 0.0)
    dsend[...] = jnp.broadcast_to(jnp.exp(c_last) * across(whole, DK // 128), (8, DK))
    for k in range(1, GROUP):
        remote(dsend, dgat.at[g], d_send.at[k], d_recv.at[g], z * GROUP + mate(k), y).start()
    dgat[g] = dsend[...]

    def conv(r0, n, source, base, c0, width, taps, t0):
        tw = taps[:, t0 : t0 + width].astype(F32)
        total = tw[3:4] * source[base + r0 : base + r0 + n, c0 : c0 + width]
        for lag in range(1, 4):
            window = source[base + r0 - lag : base + r0 - lag + n, c0 : c0 + width]
            total += tw[3 - lag : 4 - lag] * window * across(keep[lag - 1, r0 : r0 + n, :], width // 128)
        half = 0.5 * total
        return (half * jnp.tanh(half) + half).astype(BF16)

    def conv_all(c0, width, taps, store):
        for r0 in [8, 16] + list(range(32, SEG, 32)):
            n = 8 if r0 == 8 else 16 if r0 == 16 else 32
            for t0 in range(0, width, 256):
                store(r0, n, t0, conv(r0, n, ext, 8, c0 + t0, 256, taps, t0))

    def conv_first(c0, width, taps, store):
        for t0 in range(0, width, 256):
            store(0, 8, t0, conv(0, 8, ext, 8, c0 + t0, 256, taps, t0))

    def store_k(r0, n, t0, value):
        convk[r0 : r0 + n, t0 : t0 + 256] = value.astype(F32)

    def store_v(r0, n, t0, value):
        convv[r0 : r0 + n, t0 : t0 + 256] = value.astype(F32)

    conv_all(DK, DK, taps_k, store_k)
    conv_all(2 * DK, DV, taps_v, store_v)

    remote(ext.at[SEG : SEG + 8], halo, halo_sem.at[0], halo_sem.at[1], after, y).wait_recv()
    ext[0:8, :] = halo[...]
    conv_first(DK, DK, taps_k, store_k)
    conv_first(2 * DK, DV, taps_v, store_v)

    tail = jnp.where(pf_col[...] == pf_last, 1.0, 0.0)
    weighted = (convk[...] * jnp.exp(c_last - cum[...]) * across(tail, DK // 128)).astype(BF16)
    local[...] = dot_tn(weighted, convv[...].astype(BF16))
    for j in range(GROUP):
        l1s[j] = local[j * PIECE : (j + 1) * PIECE, :].astype(BF16)
    for k in range(1, GROUP):
        j = mate(k)
        remote(l1s.at[j], l1r.at[g], l1_send.at[k], l1_recv.at[g], z * GROUP + j, y).start()
    l1r[g] = l1s[g]

    for k in range(1, GROUP):
        j = mate(k)
        remote(dsend, dgat.at[j], d_send.at[k], d_recv.at[j], z * GROUP + j, y).wait_recv()
    prod = dgat[0]
    for j in range(1, GROUP):
        prod = prod * dgat[j]
    gsend[...] = prod
    for k in range(1, PLANES):
        remote(gsend, ggat.at[z], g_send.at[k], g_recv.at[z], peer(k) * GROUP + g, y).start()
    ggat[z] = gsend[...]

    def store_q(r0, n, t0, value):
        inner[r0 : r0 + n, 0:DK] = value.astype(F32)

    conv_all(0, DK, taps_q, store_q)
    conv_first(0, DK, taps_q, store_q)

    for k in range(1, PLANES):
        j = peer(k)
        remote(gsend, ggat.at[j], g_send.at[k], g_recv.at[j], j * GROUP + g, y).wait_recv()
    sub = lax.broadcasted_iota(jnp.int32, (8, DK), 0)
    d8 = dgat[0]
    g8 = ggat[0]
    for j in range(1, 8):
        d8 = jnp.where(sub == j, dgat[j], d8)
        g8 = jnp.where(sub == j, ggat[j], g8)
    dmat[...] = jnp.zeros_like(dmat)
    dmat[0:8, :] = d8
    dmat[8:16, :] = g8
    dmat[16:24, :] = dsend[...]
    dt[...] = jnp.transpose(dmat[...])

    for k in range(1, GROUP):
        j = mate(k)
        remote(l1s.at[j], l1r.at[j], l1_send.at[k], l1_recv.at[j], z * GROUP + j, y).wait_recv()
    mine = dt[pl.ds(pl.multiple_of(g * PIECE, PIECE), PIECE), :]
    run = l1r[0].astype(F32)
    for j in range(1, GROUP):
        p1[j - 1] = run
        run = run * mine[:, j : j + 1] + l1r[j].astype(F32)
    total = run.astype(BF16)
    for k in range(PLANES):
        t2s[k] = total[16 * (k // 4) : 16 * (k // 4) + 16, 128 * (k % 4) : 128 * (k % 4) + 128]
    for k in range(1, PLANES):
        j = peer(k)
        remote(t2s.at[j], t2r.at[z], t2_send.at[k], t2_recv.at[z], j * GROUP + g, y).start()
    t2r[z] = t2s[z]

    for b in range(SEG // ROWS):
        r0, r1 = b * ROWS, (b + 1) * ROWS
        q = inner[r0:r1, 0:DK]
        if b == 0:
            start = jnp.zeros((1, DK), F32)
        else:
            start = cum[r0 - 1 : r0, :]
        up_q = q * jnp.exp(cum[r0:r1, :] - start)
        intact = jnp.where(pf_col[r0:r1, :] < first, 1.0, 0.0)
        lifted[b] = (up_q * jnp.exp(start) * across(intact, DK // 128)).astype(BF16)
        down_k = (convk[0:r1, :] * jnp.exp(start - cum[0:r1, :])).astype(BF16)
        scores = dot_nt(up_q.astype(BF16), down_k)
        ri = r0 + lax.broadcasted_iota(jnp.int32, (ROWS, r1), 0)
        ci = lax.broadcasted_iota(jnp.int32, (ROWS, r1), 1)
        same = pf_col[r0:r1, 0:1] == pf_row[0:1, 0:r1]
        scores = jnp.where((ri >= ci) & same, scores, 0.0).astype(BF16)
        inner[r0:r1, :] = dot(scores, convv[0:r1, :].astype(BF16))

    for k in range(1, PLANES):
        j = peer(k)
        remote(t2s.at[j], t2r.at[j], t2_send.at[k], t2_recv.at[j], j * GROUP + g, y).wait_recv()
    tile_rows = pl.ds(pl.multiple_of(g * PIECE + 16 * lax.div(z, 4), 16), 16)
    mine2 = dt[tile_rows, :]
    run2 = jnp.zeros((16, 128), F32)
    for j in range(PLANES):
        q2s[j] = run2.astype(BF16)
        run2 = run2 * mine2[:, 8 + j : 9 + j] + t2r[j].astype(F32)
    for k in range(1, PLANES):
        j = peer(k)
        remote(q2s.at[j], q2r.at[z], q2_send.at[k], q2_recv.at[z], j * GROUP + g, y).start()
    q2r[z] = q2s[z]

    for b in range(SEG // ROWS):
        gate = acc[b, :, QKV:WIDE].astype(BF16).astype(F32)
        half = 0.5 * gate
        gg[b] = (half * jnp.tanh(half) + half) * gain_v[...]

    for k in range(1, PLANES):
        j = peer(k)
        remote(q2s.at[j], q2r.at[j], q2_send.at[k], q2_recv.at[j], j * GROUP + g, y).wait_recv()
    entry = jnp.concatenate(
        [jnp.concatenate([q2r[4 * a + c].astype(F32) for c in range(4)], axis=1) for a in range(2)],
        axis=0,
    )
    e1s[0] = entry.astype(BF16)
    for j in range(1, GROUP):
        entry = entry * mine[:, j - 1 : j]
        e1s[j] = (p1[j - 1] + entry).astype(BF16)
    for k in range(1, GROUP):
        j = mate(k)
        remote(e1s.at[j], er.at[g], e1_send.at[k], e1_recv.at[g], z * GROUP + j, y).start()
    er[g] = e1s[g]
    for k in range(1, GROUP):
        j = mate(k)
        remote(e1s.at[j], er.at[j], e1_send.at[k], e1_recv.at[j], z * GROUP + j, y).wait_recv()

    def heads(block):
        rows = pl.ds(pl.multiple_of(block * ROWS, ROWS), ROWS)
        out = inner[rows, :] + dot(lifted[block], er[...].reshape(DK, DV))
        scale = lax.rsqrt(jnp.mean(out * out, axis=1, keepdims=True) + 1e-05)
        return (out * scale * gg[block]).astype(BF16)

    def project(gated, c):
        return dot(gated, wo[:, c * CHUNK : (c + 1) * CHUNK])

    def to_right(slot, dst, sem):
        return remote(rs_s.at[slot], dst, rs_send.at[slot], sem, tok, right)

    def to_left(slot, dst, sem):
        return remote(rs_s.at[slot], dst, rs_send.at[slot], sem, tok, left)

    gated = heads(opp)
    for c in (0, 2, 1, 3):
        rs_s[c] = project(gated, c).astype(BF16)
        (to_right if c < 2 else to_left)(c, relay.at[c], relay_recv.at[c]).start()
    gated_r = heads(right)
    gated_l = heads(left)
    for i in range(2):
        c = 2 + i
        rs_s[4 + c] = project(gated_r, c).astype(BF16)
        to_right(4 + c, fl.at[c], fl_recv.at[c]).start()
        c = i
        rs_s[4 + c] = project(gated_l, c).astype(BF16)
        to_left(4 + c, fr.at[c], fr_recv.at[c]).start()
    for i in range(2):
        c = i
        part = project(gated_r, c)
        to_right(c, relay.at[c], relay_recv.at[c]).wait_recv()
        rs_s[8 + c] = (part + relay[c].astype(F32)).astype(BF16)
        to_right(8 + c, fl.at[c], fl_recv.at[c]).start()
        c = 2 + i
        part = project(gated_l, c)
        to_left(c, relay.at[c], relay_recv.at[c]).wait_recv()
        rs_s[8 + c] = (part + relay[c].astype(F32)).astype(BF16)
        to_left(8 + c, fr.at[c], fr_recv.at[c]).start()

    states[...] = er[...].reshape(DK, DV).astype(F32) * dt[:, 16:17] + local[...]
    for j in range(3):
        r = SEG - 3 + j
        inside = jnp.where(first + r >= pf_last, 1.0, 0.0)
        edges[0, j] = (ext[8 + r : 9 + r, :] * across(inside, QKV // 128)).astype(BF16)

    gated = heads(y)
    for c in (2, 3, 0, 1):
        part = project(gated, c)
        to_right(0, fl.at[c], fl_recv.at[c]).wait_recv()
        to_right(0, fr.at[c], fr_recv.at[c]).wait_recv()
        mixed[:, c * CHUNK : (c + 1) * CHUNK] = (
            part + fl[c].astype(F32) + fr[c].astype(F32)
        ).astype(BF16)

    for s in range(4):
        own_to_right(s).wait_send()
        own_to_left(s).wait_send()
    for f in range(2):
        on_to_right(f).wait_send()
        on_to_left(f).wait_send()
    halo_copy.wait_send()
    for k in range(1, 8):
        remote(dsend, dgat.at[g], d_send.at[k], d_recv.at[g], tok, y).wait_send()
        remote(gsend, ggat.at[z], g_send.at[k], g_recv.at[z], tok, y).wait_send()
        remote(l1s.at[0], l1r.at[g], l1_send.at[k], l1_recv.at[g], tok, y).wait_send()
        remote(t2s.at[0], t2r.at[z], t2_send.at[k], t2_recv.at[z], tok, y).wait_send()
        remote(q2s.at[0], q2r.at[z], q2_send.at[k], q2_recv.at[z], tok, y).wait_send()
        remote(e1s.at[0], er.at[g], e1_send.at[k], e1_recv.at[g], tok, y).wait_send()
    for slot in range(12):
        to_right(slot, fl.at[0], fl_recv.at[0]).wait_send()


def shards(
    tokens,
    prompt_lengths,
    query_weight,
    key_weight,
    value_weight,
    query_conv,
    key_conv,
    value_conv,
    decay_down,
    decay_up,
    decay_bias,
    gate_weight,
    norm_gain,
    out_weight,
):
    rank = decay_down.shape[1]
    dma = pltpu.SemaphoreType.DMA
    anywhere = pl.BlockSpec(memory_space=pl.ANY)
    vmem = pl.BlockSpec(memory_space=pltpu.VMEM)
    mixed, states, edges = pl.pallas_call(
        kernel,
        out_shape=(
            jax.ShapeDtypeStruct((ROWS, D), BF16),
            jax.ShapeDtypeStruct((DK, DV), F32),
            jax.ShapeDtypeStruct((1, 3, 1, QKV), BF16),
        ),
        in_specs=[anywhere] * 14,
        out_specs=(vmem, vmem, vmem),
        scratch_shapes=[
            pltpu.VMEM((HV, ROWS, D), BF16),
            pltpu.VMEM((D, WIDE), BF16),
            pltpu.VMEM((D, rank), BF16),
            pltpu.VMEM((DV, D), BF16),
            pltpu.VMEM((4, DK), BF16),
            pltpu.VMEM((4, DK), BF16),
            pltpu.VMEM((4, DV), BF16),
            pltpu.VMEM((rank, DK), BF16),
            pltpu.VMEM((1, DK), F32),
            pltpu.VMEM((1, DV), F32),
            pltpu.SMEM(prompt_lengths.shape, jnp.int32),
            pltpu.VMEM((HV, ROWS, WIDE), F32),
            pltpu.VMEM((HV, ROWS, rank), F32),
            pltpu.VMEM((8 + SEG, QKV), F32),
            pltpu.VMEM((8, QKV), F32),
            pltpu.VMEM((SEG, 128), jnp.int32),
            pltpu.VMEM((8, SEG), jnp.int32),
            pltpu.VMEM((3, SEG, 128), F32),
            pltpu.VMEM((SEG, DK), F32),
            pltpu.VMEM((SEG, DK), F32),
            pltpu.VMEM((SEG, DV), F32),
            pltpu.VMEM((DK, DV), F32),
            pltpu.VMEM((HV, ROWS, DK), BF16),
            pltpu.VMEM((SEG, DV), F32),
            pltpu.VMEM((HV, ROWS, DV), F32),
            pltpu.VMEM((8, DK), F32),
            pltpu.VMEM((GROUP, 8, DK), F32),
            pltpu.VMEM((8, DK), F32),
            pltpu.VMEM((PLANES, 8, DK), F32),
            pltpu.VMEM((128, DK), F32),
            pltpu.VMEM((DK, 128), F32),
            pltpu.VMEM((GROUP, PIECE, DV), BF16),
            pltpu.VMEM((GROUP, PIECE, DV), BF16),
            pltpu.VMEM((GROUP - 1, PIECE, DV), F32),
            pltpu.VMEM((PLANES, 16, 128), BF16),
            pltpu.VMEM((PLANES, 16, 128), BF16),
            pltpu.VMEM((PLANES, 16, 128), BF16),
            pltpu.VMEM((PLANES, 16, 128), BF16),
            pltpu.VMEM((GROUP, PIECE, DV), BF16),
            pltpu.VMEM((GROUP, PIECE, DV), BF16),
            pltpu.VMEM((12, ROWS, CHUNK), BF16),
            pltpu.VMEM((4, ROWS, CHUNK), BF16),
            pltpu.VMEM((4, ROWS, CHUNK), BF16),
            pltpu.VMEM((4, ROWS, CHUNK), BF16),
            dma((4, 4)),
            dma((10,)),
            dma((2, 6)),
            dma((2, 6)),
            dma((2,)),
            dma((8,)),
            dma((8,)),
            dma((8,)),
            dma((8,)),
            dma((8,)),
            dma((8,)),
            dma((8,)),
            dma((8,)),
            dma((8,)),
            dma((8,)),
            dma((8,)),
            dma((8,)),
            dma((12,)),
            dma((4,)),
            dma((4,)),
            dma((4,)),
        ],
        compiler_params=pltpu.CompilerParams(
            collective_id=0, has_side_effects=True, vmem_limit_bytes=48 * 1024 * 1024
        ),
        name="gla",
    )(
        tokens,
        prompt_lengths,
        query_weight,
        key_weight,
        value_weight,
        query_conv,
        key_conv,
        value_conv,
        decay_down,
        decay_up,
        decay_bias.reshape(1, DK),
        gate_weight,
        norm_gain.reshape(1, DV),
        out_weight,
    )
    return mixed, states[None, None], edges


def solution(mesh):
    in_specs = (
        P(("tok", "hv"), None),
        P(),
        P(None, "hv"),
        P(None, "hv"),
        P(None, "hv"),
        P(None, "hv"),
        P(None, "hv"),
        P(None, "hv"),
        P(),
        P(None, "hv"),
        P("hv"),
        P(None, "hv"),
        P(),
        P("hv", None),
    )
    out_specs = (P(("tok", "hv"), None), P("tok", "hv", None, None), P("tok", None, "hv", None))
    return jax.shard_map(shards, mesh=mesh, in_specs=in_specs, out_specs=out_specs, check_vma=False)
```

time: 353 us -> 71.8 us (0.20); the launches traced: 348 us -> 71.4 us
  waiting for transfers between devices: 217 us -> 0 us
  Pallas kernels: 0 us -> 57.7 us
  blocking collectives: 45.6 us -> 0 us
  matrix products: 24.7 us -> 0 us
  other arithmetic: 23.3 us -> 0 us
  between operations: 14 us -> 0.66 us
  starting transfers between devices: 4.67 us -> 0 us
    all_gather x2 -> x0, waiting for transfers between devices: 121 us -> none  [the longest x1 95.1 us: carried_in(): gathered = jax.tree.map(lambda a: lax.all_gather(a, axis), part)]
    reduce_scatter x1 -> x0, waiting for transfers between devices: 96 us -> none  [shards(): lax.psum_scatter(jnp.dot(gated_out, out_weight, preferred_element_type=jn...]
    pallas_call x0 -> x1, Pallas kernels: none -> 57.7 us  [shards(): pl.pallas_call(kernel, out_shape=(jax.ShapeDtypeStruct((ROWS, D), BF16),...]
    all_gather x1 -> x0, blocking collectives: 45.6 us -> none  [carried_in(): gathered = jax.tree.map(lambda a: lax.all_gather(a, axis), part)]
    dot_general x22 -> x0, matrix products: 24.7 us -> none  [the longest x4 7.52 us: span_step(): jnp.dot(lifted * intact[:, None], memory, precision=HIGHEST_PRECISION)]
    unnamed x27 -> x26, local copies, waits for them, and re-layouts: 0.86 us -> 13 us
    convert_element_type x13 -> x0, other arithmetic: 10.7 us -> none  [the longest x8 5.59 us: span_parts(): in_tail = (groups == groups[-1]).astype(jnp.float32)]
    slice x23 -> x0, local copies, waits for them, and re-layouts: 7.67 us -> none  [the longest x8 4.39 us: span_parts(): step_decay = jnp.exp(final_log) * intact[-1]]
  transfers between devices with their start and end apart: 4 -> 0, of which waited for: 3 -> 0; matrix products, arithmetic and copies ran while one was open for 3% -> 0% of each run, Pallas kernels for 0% -> 0%
where the time goes in v1:
time: 71.8 us; the launch traced here: 71.4 us
  Pallas kernels  57.7 us (80%)
  local copies, waits for them, and re-layouts  13 us (18%)
    pallas_call x1, Pallas kernels, shards(): pl.pallas_call(kernel, out_shape=(jax.ShapeDtypeStruct((ROWS, D), BF16),...  57.7 us
    unnamed x26, local copies, waits for them, and re-layouts  13 us

profile of v1, /device:TPU:1, one launch (start us, length us, event | category | flops | bytes accessed | tf_op | source)
XLA Modules:
  0.0 71.4 jit_solution(3702863998173249052)
XLA Ops:
  0.6 1.1 %copy.17.wdown = bf16[2048,16]{1,0:T(8,128)(2,1)S(1)} copy(bf16[2048,16]{0,1:T(8,128)(2,1)} %param.22) | data formatting | bytes 131072 | tf_op args[8]
  1.7 0.0 copy-start
  1.8 1.6 %copy-done = bf16[2048,512]{1,0:T(8,128)(2,1)S(1)} copy-done((bf16[2048,512]{1,0:T(8,128)(2,1)S(1)}, bf16[2048,512]{1,0:T(8,128)(2,1)}, u32[]{:S(2)}) %copy-start) | copy-done | bytes 2097176
  3.3 0.0 copy-start.1
  3.3 1.2 %copy-done.1 = bf16[2048,256]{1,0:T(8,128)(2,1)S(1)} copy-done((bf16[2048,256]{1,0:T(8,128)(2,1)S(1)}, bf16[2048,256]{1,0:T(8,128)(2,1)}, u32[]{:S(2)}) %copy-start.1) | copy-done | bytes 1048600
  4.6 0.0 copy-start.2
  4.6 1.2 %copy-done.2 = bf16[2048,256]{1,0:T(8,128)(2,1)S(1)} copy-done((bf16[2048,256]{1,0:T(8,128)(2,1)S(1)}, bf16[2048,256]{1,0:T(8,128)(2,1)}, u32[]{:S(2)}) %copy-start.2) | copy-done | bytes 1048600
  5.8 0.0 copy-start.3
  5.8 0.9 %copy-done.3 = bf16[64,2048]{1,0:T(8,128)(2,1)S(1)} copy-done((bf16[64,2048]{1,0:T(8,128)(2,1)S(1)}, bf16[64,2048]{1,0:T(8,128)(2,1)}, u32[]{:S(2)}) %copy-start.3) | copy-done | bytes 262168
  6.7 0.0 copy-start.4
  6.7 0.7 copy-done.4
  7.4 0.0 copy-start.5
  7.4 0.7 copy-done.5
  8.1 0.0 copy-start.6
  8.1 0.7 copy-done.6
  8.8 0.0 copy-start.7
  8.8 0.7 copy-done.7
  9.5 0.0 copy-start.8
  9.5 0.7 copy-done.8
  10.2 0.0 copy-start.9
  10.2 0.7 copy-done.9
  10.9 0.0 copy-start.10
  10.9 0.7 copy-done.10
  11.5 57.7 %gla.1 = (bf16[64,2048]{1,0:T(8,128)(2,1)S(1)}, f32[256,512]{1,0:T(8,128)S(1)}, bf16[1,3,1,1024]{3,2,1,0:T(2,128)(2,1)S(1)}) custom-call(bf16[64,2048]{1,0:T(8,128)(2,1)S(1)} %copy-done.3, s32[33]{0:T(128)S(1)} %copy-done.10, bf16[2048,256]{1,0:T(8,128)(2,1)S(1)} %copy-done.1, bf16[2048,256]{1,0:T(8,128)(2,1)S(1)} %copy-done.2, ...), custom_call_target="tpu_custom_call" | custom-call | tf_op jit(solution)/shard_map/gla/pallas_call | solution.py:577
  69.3 0.6 copy.18
  69.9 0.7 copy.21
  70.6 0.8 %copy.22 = f32[1,1,256,512]{3,2,1,0:T(8,128)} copy(f32[1,1,256,512]{3,2,1,0:T(8,128)S(1)} %bitcast.3) | data formatting | bytes 1048576
Async XLA Ops:
  1.7 1.6 %copy-start = (bf16[2048,512]{1,0:T(8,128)(2,1)S(1)}, bf16[2048,512]{1,0:T(8,128)(2,1)}, u32[]{:S(2)}) copy-start(bf16[2048,512]{1,0:T(8,128)(2,1)} %wv.1) | copy-start | bytes 6291460
  3.3 1.2 %copy-start.1 = (bf16[2048,256]{1,0:T(8,128)(2,1)S(1)}, bf16[2048,256]{1,0:T(8,128)(2,1)}, u32[]{:S(2)}) copy-start(bf16[2048,256]{1,0:T(8,128)(2,1)} %wq.1) | copy-start | bytes 3145732
  4.6 1.2 %copy-start.2 = (bf16[2048,256]{1,0:T(8,128)(2,1)S(1)}, bf16[2048,256]{1,0:T(8,128)(2,1)}, u32[]{:S(2)}) copy-start(bf16[2048,256]{1,0:T(8,128)(2,1)} %wk.1) | copy-start | bytes 3145732
  5.8 0.9 %copy-start.3 = (bf16[64,2048]{1,0:T(8,128)(2,1)S(1)}, bf16[64,2048]{1,0:T(8,128)(2,1)}, u32[]{:S(2)}) copy-start(bf16[64,2048]{1,0:T(8,128)(2,1)} %tokens.1) | copy-start | bytes 786436
  6.7 0.7 copy-start.4
  7.4 0.7 copy-start.5
  8.1 0.7 copy-start.6
  8.8 0.7 copy-start.7
  9.5 0.7 copy-start.8
  10.2 0.7 copy-start.9
  10.9 0.7 copy-start.10

commit v2 on v1

--- a/solution.py
+++ b/solution.py
@@ -23,7 +23,13 @@
 QKV = 2 * DK + DV
 WIDE = QKV + DV
 CHUNK = 512
-PIECE = DK // GROUP
+HALF = DK // 2
+XS = 4
+CHIPS = XS * PLANES
+OTHERS = sorted(
+    [(dz, dx) for dz in range(PLANES) for dx in range(XS) if (dz, dx) != (0, 0)],
+    key=lambda d: -(min(d[0], PLANES - d[0]) + min(d[1], XS - d[1])),
+)
 
 
 def dot(a, b):
@@ -90,15 +96,16 @@
     gsend,
     ggat,
     dmat,
+    dts,
     dt,
-    l1s,
-    l1r,
-    p1,
-    t2s,
-    t2r,
-    q2s,
-    q2r,
-    e1s,
+    pair_s,
+    pair_r,
+    first_l,
+    ts,
+    tr,
+    qs,
+    qr,
+    pe_s,
     er,
     rs_s,
     relay,
@@ -113,14 +120,12 @@
     d_recv,
     g_send,
     g_recv,
-    l1_send,
-    l1_recv,
-    t2_send,
-    t2_recv,
-    q2_send,
-    q2_recv,
-    e1_send,
-    e1_recv,
+    pair_sem,
+    t_send,
+    t_recv,
+    q_send,
+    q_recv,
+    pe_sem,
     rs_send,
     relay_recv,
     fl_recv,
@@ -131,6 +136,9 @@
     n_tok = GROUP * PLANES
     z = lax.div(tok, GROUP)
     g = lax.rem(tok, GROUP)
+    x = lax.div(g, 2)
+    core = lax.rem(tok, 2)
+    sib = tok + 1 - 2 * core
     right = lax.rem(y + 1, HV)
     left = lax.rem(y + HV - 1, HV)
     opp = lax.rem(y + 2, HV)
@@ -147,6 +155,10 @@
 
     def peer(k):
         return lax.rem(z + k, PLANES)
+
+    def chip(d):
+        other_z, other_x = lax.rem(z + d[0], PLANES), lax.rem(x + d[1], XS)
+        return other_z * XS + other_x, other_z * GROUP + other_x * 2 + core
 
     own = pltpu.make_async_copy(tokens, xt.at[y], loc_sem.at[0])
     own.start()
@@ -184,8 +196,8 @@
     pl.semaphore_signal(barrier, inc=1, device_id=(before, y), device_id_type=MESH)
     for k in range(1, GROUP):
         pl.semaphore_signal(barrier, inc=1, device_id=(z * GROUP + mate(k), y), device_id_type=MESH)
-    for k in range(1, PLANES):
-        pl.semaphore_signal(barrier, inc=1, device_id=(peer(k) * GROUP + g, y), device_id_type=MESH)
+    for d in OTHERS:
+        pl.semaphore_signal(barrier, inc=1, device_id=(chip(d)[1], y), device_id_type=MESH)
     for copy in small[:2]:
         copy.start()
     for c in range(D // CHUNK):
@@ -193,7 +205,7 @@
             copy.start()
     for copy in small[2:]:
         copy.start()
-    pl.semaphore_wait(barrier, 4 + GROUP - 1 + PLANES - 1)
+    pl.semaphore_wait(barrier, 4 + GROUP - 1 + len(OTHERS))
 
     def cols(c):
         return pl.ds(pl.multiple_of(c * CHUNK, CHUNK), CHUNK)
@@ -267,7 +279,7 @@
         x = xt[block, :, cols(c)]
         for n in range(0, WIDE, CHUNK):
             acc[block, :, n : n + CHUNK] += dot(x, wall[cols(c), n : n + CHUNK])
-        accl[block] += dot(x, wlow[cols(c), :])
+        accl[block] += dot_nt(x, wlow[:, cols(c)])
 
     own.wait()
 
@@ -330,8 +342,11 @@
     pf_last = pf_col[SEG - 1 : SEG, :]
     whole = jnp.where(pf_last < first, 1.0, 0.0)
     dsend[...] = jnp.broadcast_to(jnp.exp(c_last) * across(whole, DK // 128), (8, DK))
-    for k in range(1, GROUP):
-        remote(dsend, dgat.at[g], d_send.at[k], d_recv.at[g], z * GROUP + mate(k), y).start()
+    remote(dsend, dgat.at[g], d_send.at[0], d_recv.at[g], sib, y).start()
+    for dx in (2, 1, 3):
+        for dc in range(2):
+            to = z * GROUP + lax.rem(x + dx, XS) * 2 + lax.rem(core + dc, 2)
+            remote(dsend, dgat.at[g], d_send.at[2 * dx + dc], d_recv.at[g], to, y).start()
     dgat[g] = dsend[...]
 
     def conv(r0, n, source, base, c0, width, taps, t0):
@@ -370,21 +385,57 @@
     tail = jnp.where(pf_col[...] == pf_last, 1.0, 0.0)
     weighted = (convk[...] * jnp.exp(c_last - cum[...]) * across(tail, DK // 128)).astype(BF16)
     local[...] = dot_tn(weighted, convv[...].astype(BF16))
-    for j in range(GROUP):
-        l1s[j] = local[j * PIECE : (j + 1) * PIECE, :].astype(BF16)
-    for k in range(1, GROUP):
-        j = mate(k)
-        remote(l1s.at[j], l1r.at[g], l1_send.at[k], l1_recv.at[g], z * GROUP + j, y).start()
-    l1r[g] = l1s[g]
-
-    for k in range(1, GROUP):
-        j = mate(k)
-        remote(dsend, dgat.at[j], d_send.at[k], d_recv.at[j], z * GROUP + j, y).wait_recv()
-    prod = dgat[0]
-    for j in range(1, GROUP):
-        prod = prod * dgat[j]
-    gsend[...] = prod
-    for k in range(1, PLANES):
+
+    def half_rows(which):
+        return pl.ds(pl.multiple_of(which * HALF, HALF), HALF)
+
+    pair_s[...] = local[half_rows(1 - core), :].astype(BF16)
+    to_sib = remote(pair_s, pair_r, pair_sem.at[0], pair_sem.at[1], sib, y)
+    to_sib.start()
+    sib_g = g + 1 - 2 * core
+    remote(dsend, dgat.at[sib_g], d_send.at[0], d_recv.at[sib_g], sib, y).wait_recv()
+    dmat[0:8, :] = dsend[...]
+    dmat[8:16, :] = dgat[sib_g]
+    dts[...] = jnp.transpose(dmat[...])
+    mine_d = dts[half_rows(core), :]
+    own_d, sib_d = mine_d[:, 0:1], mine_d[:, 8:9]
+    is_first = core == 0
+    d_first = jnp.where(is_first, own_d, sib_d)
+    d_second = jnp.where(is_first, sib_d, own_d)
+    to_sib.wait_recv()
+    own_l = local[half_rows(core), :]
+    sib_l = pair_r[...].astype(F32)
+    l_first = jnp.where(is_first, own_l, sib_l)
+    first_l[...] = l_first
+    chip_l = (l_first * d_second + jnp.where(is_first, sib_l, own_l)).astype(BF16)
+    for k in range(CHIPS):
+        ts[k] = chip_l[16 * (k // XS) : 16 * (k // XS) + 16, 128 * (k % XS) : 128 * (k % XS) + 128]
+    me = z * XS + x
+
+    def to_chip(i, d, src, dst, ss, rs):
+        k, device = chip(d)
+        return remote(src.at[k], dst.at[me], ss.at[i], rs.at[me], device, y)
+
+    def from_chip(d, dst, ss, rs):
+        k, device = chip(d)
+        return remote(dst.at[k], dst.at[k], ss.at[0], rs.at[k], device, y)
+
+    for i, d in enumerate(OTHERS):
+        to_chip(i, d, ts, tr, t_send, t_recv).start()
+    tr[me] = ts[me]
+
+    for dx in (1, 3, 2):
+        for dc in range(2):
+            j = lax.rem(x + dx, XS) * 2 + lax.rem(core + dc, 2)
+            remote(dsend, dgat.at[j], d_send.at[0], d_recv.at[j], z * GROUP + j, y).wait_recv()
+
+    sub = lax.broadcasted_iota(jnp.int32, (8, HALF), 0)
+    chips_d = jnp.zeros((8, HALF), F32)
+    for j in range(XS):
+        both = dgat[2 * j] * dgat[2 * j + 1]
+        chips_d = jnp.where(sub == j, jnp.where(is_first, both[:, 0:HALF], both[:, HALF:DK]), chips_d)
+    gsend[...] = chips_d
+    for k in (4, 3, 5, 2, 6, 1, 7):
         remote(gsend, ggat.at[z], g_send.at[k], g_recv.at[z], peer(k) * GROUP + g, y).start()
     ggat[z] = gsend[...]
 
@@ -393,37 +444,6 @@
 
     conv_all(0, DK, taps_q, store_q)
     conv_first(0, DK, taps_q, store_q)
-
-    for k in range(1, PLANES):
-        j = peer(k)
-        remote(gsend, ggat.at[j], g_send.at[k], g_recv.at[j], j * GROUP + g, y).wait_recv()
-    sub = lax.broadcasted_iota(jnp.int32, (8, DK), 0)
-    d8 = dgat[0]
-    g8 = ggat[0]
-    for j in range(1, 8):
-        d8 = jnp.where(sub == j, dgat[j], d8)
-        g8 = jnp.where(sub == j, ggat[j], g8)
-    dmat[...] = jnp.zeros_like(dmat)
-    dmat[0:8, :] = d8
-    dmat[8:16, :] = g8
-    dmat[16:24, :] = dsend[...]
-    dt[...] = jnp.transpose(dmat[...])
-
-    for k in range(1, GROUP):
-        j = mate(k)
-        remote(l1s.at[j], l1r.at[j], l1_send.at[k], l1_recv.at[j], z * GROUP + j, y).wait_recv()
-    mine = dt[pl.ds(pl.multiple_of(g * PIECE, PIECE), PIECE), :]
-    run = l1r[0].astype(F32)
-    for j in range(1, GROUP):
-        p1[j - 1] = run
-        run = run * mine[:, j : j + 1] + l1r[j].astype(F32)
-    total = run.astype(BF16)
-    for k in range(PLANES):
-        t2s[k] = total[16 * (k // 4) : 16 * (k // 4) + 16, 128 * (k % 4) : 128 * (k % 4) + 128]
-    for k in range(1, PLANES):
-        j = peer(k)
-        remote(t2s.at[j], t2r.at[z], t2_send.at[k], t2_recv.at[z], j * GROUP + g, y).start()
-    t2r[z] = t2s[z]
 
     for b in range(SEG // ROWS):
         r0, r1 = b * ROWS, (b + 1) * ROWS
@@ -434,7 +454,9 @@
             start = cum[r0 - 1 : r0, :]
         up_q = q * jnp.exp(cum[r0:r1, :] - start)
         intact = jnp.where(pf_col[r0:r1, :] < first, 1.0, 0.0)
-        lifted[b] = (up_q * jnp.exp(start) * across(intact, DK // 128)).astype(BF16)
+        reach = (up_q * jnp.exp(start) * across(intact, DK // 128)).astype(BF16)
+        lifted[0, b] = reach[:, 0:HALF]
+        lifted[1, b] = reach[:, HALF:DK]
         down_k = (convk[0:r1, :] * jnp.exp(start - cum[0:r1, :])).astype(BF16)
         scores = dot_nt(up_q.astype(BF16), down_k)
         ri = r0 + lax.broadcasted_iota(jnp.int32, (ROWS, r1), 0)
@@ -445,45 +467,45 @@
 
     for k in range(1, PLANES):
         j = peer(k)
-        remote(t2s.at[j], t2r.at[j], t2_send.at[k], t2_recv.at[j], j * GROUP + g, y).wait_recv()
-    tile_rows = pl.ds(pl.multiple_of(g * PIECE + 16 * lax.div(z, 4), 16), 16)
-    mine2 = dt[tile_rows, :]
-    run2 = jnp.zeros((16, 128), F32)
-    for j in range(PLANES):
-        q2s[j] = run2.astype(BF16)
-        run2 = run2 * mine2[:, 8 + j : 9 + j] + t2r[j].astype(F32)
-    for k in range(1, PLANES):
-        j = peer(k)
-        remote(q2s.at[j], q2r.at[z], q2_send.at[k], q2_recv.at[z], j * GROUP + g, y).start()
-    q2r[z] = q2s[z]
+        remote(gsend, ggat.at[j], g_send.at[k], g_recv.at[j], j * GROUP + g, y).wait_recv()
+    padded = jnp.concatenate([ggat[...].reshape(8 * PLANES, HALF), jnp.zeros((64, HALF), F32)], axis=0)
+    dt[...] = jnp.transpose(padded)
+
+    for d in OTHERS:
+        from_chip(d, tr, t_send, t_recv).wait_recv()
+    tile_d = dt[pl.ds(pl.multiple_of(16 * z, 16), 16), :]
+    run = jnp.zeros((16, 128), F32)
+    for k in range(CHIPS):
+        qs[k] = run.astype(BF16)
+        lane = 8 * (k // XS) + k % XS
+        run = run * tile_d[:, lane : lane + 1] + tr[k].astype(F32)
+    for i, d in enumerate(OTHERS):
+        to_chip(i, d, qs, qr, q_send, q_recv).start()
+    qr[me] = qs[me]
 
     for b in range(SEG // ROWS):
         gate = acc[b, :, QKV:WIDE].astype(BF16).astype(F32)
         half = 0.5 * gate
         gg[b] = (half * jnp.tanh(half) + half) * gain_v[...]
 
-    for k in range(1, PLANES):
-        j = peer(k)
-        remote(q2s.at[j], q2r.at[j], q2_send.at[k], q2_recv.at[j], j * GROUP + g, y).wait_recv()
-    entry = jnp.concatenate(
-        [jnp.concatenate([q2r[4 * a + c].astype(F32) for c in range(4)], axis=1) for a in range(2)],
+    for d in OTHERS:
+        from_chip(d, qr, q_send, q_recv).wait_recv()
+    at_first = jnp.concatenate(
+        [jnp.concatenate([qr[XS * a + b].astype(F32) for b in range(XS)], axis=1) for a in range(PLANES)],
         axis=0,
     )
-    e1s[0] = entry.astype(BF16)
-    for j in range(1, GROUP):
-        entry = entry * mine[:, j - 1 : j]
-        e1s[j] = (p1[j - 1] + entry).astype(BF16)
-    for k in range(1, GROUP):
-        j = mate(k)
-        remote(e1s.at[j], er.at[g], e1_send.at[k], e1_recv.at[g], z * GROUP + j, y).start()
-    er[g] = e1s[g]
-    for k in range(1, GROUP):
-        j = mate(k)
-        remote(e1s.at[j], er.at[j], e1_send.at[k], e1_recv.at[j], z * GROUP + j, y).wait_recv()
+    at_second = at_first * d_first + first_l[...]
+    pe_s[...] = jnp.where(is_first, at_second, at_first).astype(BF16)
+    sib_e = remote(pe_s, er.at[core], pe_sem.at[0], pe_sem.at[1], sib, y)
+    sib_e.start()
+    er[core] = jnp.where(is_first, at_first, at_second).astype(BF16)
+    for b in range(SEG // ROWS):
+        inner[b * ROWS : (b + 1) * ROWS, :] += dot(lifted[core, b], er[core])
+    remote(pe_s, er.at[1 - core], pe_sem.at[0], pe_sem.at[1], sib, y).wait_recv()
 
     def heads(block):
         rows = pl.ds(pl.multiple_of(block * ROWS, ROWS), ROWS)
-        out = inner[rows, :] + dot(lifted[block], er[...].reshape(DK, DV))
+        out = inner[rows, :] + dot(lifted[1 - core, block], er[1 - core])
         scale = lax.rsqrt(jnp.mean(out * out, axis=1, keepdims=True) + 1e-05)
         return (out * scale * gg[block]).astype(BF16)
 
@@ -521,11 +543,11 @@
         rs_s[8 + c] = (part + relay[c].astype(F32)).astype(BF16)
         to_left(8 + c, fr.at[c], fr_recv.at[c]).start()
 
-    states[...] = er[...].reshape(DK, DV).astype(F32) * dt[:, 16:17] + local[...]
+    states[...] = er[...].reshape(DK, DV).astype(F32) * dts[:, 0:1] + local[...]
     for j in range(3):
         r = SEG - 3 + j
         inside = jnp.where(first + r >= pf_last, 1.0, 0.0)
-        edges[0, j] = (ext[8 + r : 9 + r, :] * across(inside, QKV // 128)).astype(BF16)
+        edges[0, 0, j : j + 1, :] = (ext[8 + r : 9 + r, :] * across(inside, QKV // 128)).astype(BF16)
 
     gated = heads(y)
     for c in (2, 3, 0, 1):
@@ -543,15 +565,28 @@
         on_to_right(f).wait_send()
         on_to_left(f).wait_send()
     halo_copy.wait_send()
-    for k in range(1, 8):
-        remote(dsend, dgat.at[g], d_send.at[k], d_recv.at[g], tok, y).wait_send()
-        remote(gsend, ggat.at[z], g_send.at[k], g_recv.at[z], tok, y).wait_send()
-        remote(l1s.at[0], l1r.at[g], l1_send.at[k], l1_recv.at[g], tok, y).wait_send()
-        remote(t2s.at[0], t2r.at[z], t2_send.at[k], t2_recv.at[z], tok, y).wait_send()
-        remote(q2s.at[0], q2r.at[z], q2_send.at[k], q2_recv.at[z], tok, y).wait_send()
-        remote(e1s.at[0], er.at[g], e1_send.at[k], e1_recv.at[g], tok, y).wait_send()
+    for k in [0] + list(range(2, 8)):
+        remote(dsend, dgat.at[g], d_send.at[k], d_recv.at[g], sib, y).wait_send()
+    for k in range(1, PLANES):
+        remote(gsend, ggat.at[z], g_send.at[k], g_recv.at[z], sib, y).wait_send()
+    to_sib.wait_send()
+    sib_e.wait_send()
+    for i, d in enumerate(OTHERS):
+        to_chip(i, d, ts, tr, t_send, t_recv).wait_send()
+        to_chip(i, d, qs, qr, q_send, q_recv).wait_send()
     for slot in range(12):
         to_right(slot, fl.at[0], fl_recv.at[0]).wait_send()
+
+
+def write_out(mixed, states, edges, mixed_out, states_out, edges_out, sem):
+    copies = [
+        pltpu.make_async_copy(src, dst, sem.at[i])
+        for i, (src, dst) in enumerate([(states, states_out), (mixed, mixed_out), (edges, edges_out)])
+    ]
+    for copy in copies:
+        copy.start()
+    for copy in copies:
+        copy.wait()
 
 
 def shards(
@@ -579,14 +614,14 @@
         out_shape=(
             jax.ShapeDtypeStruct((ROWS, D), BF16),
             jax.ShapeDtypeStruct((DK, DV), F32),
-            jax.ShapeDtypeStruct((1, 3, 1, QKV), BF16),
+            jax.ShapeDtypeStruct((1, 1, 3, QKV), BF16),
         ),
         in_specs=[anywhere] * 14,
         out_specs=(vmem, vmem, vmem),
         scratch_shapes=[
             pltpu.VMEM((HV, ROWS, D), BF16),
             pltpu.VMEM((D, WIDE), BF16),
-            pltpu.VMEM((D, rank), BF16),
+            pltpu.VMEM((rank, D), BF16),
             pltpu.VMEM((DV, D), BF16),
             pltpu.VMEM((4, DK), BF16),
             pltpu.VMEM((4, DK), BF16),
@@ -606,24 +641,25 @@
             pltpu.VMEM((SEG, DK), F32),
             pltpu.VMEM((SEG, DV), F32),
             pltpu.VMEM((DK, DV), F32),
-            pltpu.VMEM((HV, ROWS, DK), BF16),
+            pltpu.VMEM((2, HV, ROWS, HALF), BF16),
             pltpu.VMEM((SEG, DV), F32),
             pltpu.VMEM((HV, ROWS, DV), F32),
             pltpu.VMEM((8, DK), F32),
             pltpu.VMEM((GROUP, 8, DK), F32),
-            pltpu.VMEM((8, DK), F32),
-            pltpu.VMEM((PLANES, 8, DK), F32),
+            pltpu.VMEM((8, HALF), F32),
+            pltpu.VMEM((PLANES, 8, HALF), F32),
             pltpu.VMEM((128, DK), F32),
             pltpu.VMEM((DK, 128), F32),
-            pltpu.VMEM((GROUP, PIECE, DV), BF16),
-            pltpu.VMEM((GROUP, PIECE, DV), BF16),
-            pltpu.VMEM((GROUP - 1, PIECE, DV), F32),
-            pltpu.VMEM((PLANES, 16, 128), BF16),
-            pltpu.VMEM((PLANES, 16, 128), BF16),
-            pltpu.VMEM((PLANES, 16, 128), BF16),
-            pltpu.VMEM((PLANES, 16, 128), BF16),
-            pltpu.VMEM((GROUP, PIECE, DV), BF16),
-            pltpu.VMEM((GROUP, PIECE, DV), BF16),
+            pltpu.VMEM((HALF, 128), F32),
+            pltpu.VMEM((HALF, DV), BF16),
+            pltpu.VMEM((HALF, DV), BF16),
+            pltpu.VMEM((HALF, DV), F32),
+            pltpu.VMEM((CHIPS, 16, 128), BF16),
+            pltpu.VMEM((CHIPS, 16, 128), BF16),
+            pltpu.VMEM((CHIPS, 16, 128), BF16),
+            pltpu.VMEM((CHIPS, 16, 128), BF16),
+            pltpu.VMEM((HALF, DV), BF16),
+            pltpu.VMEM((2, HALF, DV), BF16),
             pltpu.VMEM((12, ROWS, CHUNK), BF16),
             pltpu.VMEM((4, ROWS, CHUNK), BF16),
             pltpu.VMEM((4, ROWS, CHUNK), BF16),
@@ -637,21 +673,19 @@
             dma((8,)),
             dma((8,)),
             dma((8,)),
-            dma((8,)),
-            dma((8,)),
-            dma((8,)),
-            dma((8,)),
-            dma((8,)),
-            dma((8,)),
-            dma((8,)),
-            dma((8,)),
+            dma((2,)),
+            dma((CHIPS,)),
+            dma((CHIPS,)),
+            dma((CHIPS,)),
+            dma((CHIPS,)),
+            dma((2,)),
             dma((12,)),
             dma((4,)),
             dma((4,)),
             dma((4,)),
         ],
         compiler_params=pltpu.CompilerParams(
-            collective_id=0, has_side_effects=True, vmem_limit_bytes=48 * 1024 * 1024
+            collective_id=0, has_side_effects=True, vmem_limit_bytes=63 * 1024 * 1024
         ),
         name="gla",
     )(
@@ -663,14 +697,23 @@
         query_conv,
         key_conv,
         value_conv,
-        decay_down,
+        decay_down.T,
         decay_up,
         decay_bias.reshape(1, DK),
         gate_weight,
         norm_gain.reshape(1, DV),
         out_weight,
     )
-    return mixed, states[None, None], edges
+    parts = (mixed, states, edges)
+    mixed, states, edges = pl.pallas_call(
+        write_out,
+        out_shape=tuple(jax.ShapeDtypeStruct(a.shape, a.dtype) for a in parts),
+        in_specs=[anywhere] * 3,
+        out_specs=(anywhere,) * 3,
+        scratch_shapes=[dma((3,))],
+        name="write_out",
+    )(*parts)
+    return mixed, states[None, None], edges.transpose(0, 2, 1, 3)
 
 
 def solution(mesh):

time: 71.8 us -> 81.3 us (1.13)
  Pallas kernels: 57.7 us -> 80.6 us
  local copies, waits for them, and re-layouts: 13 us -> 0 us
    pallas_call x0 -> x1, Pallas kernels: none -> 25.2 us  [shards(): pl.pallas_call(write_out, out_shape=tuple((jax.ShapeDtypeStruct(a.shape,...]
    unnamed x26 -> x0, local copies, waits for them, and re-layouts: 13 us -> none
    pallas_call x1, Pallas kernels: 57.7 us -> 55.4 us  [shards(): pl.pallas_call(kernel, out_shape=(jax.ShapeDtypeStruct((ROWS, D), BF16),...]
where the time goes in v2:
time: 81.3 us
  Pallas kernels  80.6 us (99%)
    pallas_call x1, Pallas kernels, shards(): pl.pallas_call(kernel, out_shape=(jax.ShapeDtypeStruct((ROWS, D), BF16),...  55.4 us
    pallas_call x1, Pallas kernels, shards(): pl.pallas_call(write_out, out_shape=tuple((jax.ShapeDtypeStruct(a.shape,...  25.2 us

profile of v2, /device:TPU:1, one launch (start us, length us, event | category | flops | bytes accessed | tf_op | source)
XLA Modules:
  0.0 81.3 jit_solution(15416871430843708735)
XLA Ops:
  0.6 55.4 %gla.1 = (bf16[64,2048]{1,0:T(8,128)(2,1)}, f32[256,512]{1,0:T(8,128)}, bf16[1,1,3,1024]{3,2,1,0:T(4,128)(2,1)}) custom-call(bf16[64,2048]{1,0:T(8,128)(2,1)} %tokens.1, s32[33]{0:T(128)} %lengths.1, bf16[2048,256]{1,0:T(8,128)(2,1)} %wq.1, bf16[2048,256]{1,0:T(8,128)(2,1)} %wk.1, bf16[2048,512]{1,0:T(8,128)(2,1)} %wv.1, bf16[4,256]{1,0:T(4,128)(2,1)} %cq.1, ...), custom_call_target="tpu_custom_call" | custom-call | tf_op jit(solution)/shard_map/gla/pallas_call | solution.py:612
  56.1 25.2 %write_out.1 = (bf16[64,2048]{1,0:T(8,128)(2,1)}, f32[256,512]{1,0:T(8,128)}, bf16[1,1,3,1024]{3,2,1,0:T(4,128)(2,1)}) custom-call(bf16[64,2048]{1,0:T(8,128)(2,1)} %get-tuple-element.9.mixed, f32[256,512]{1,0:T(8,128)} %get-tuple-element.10.states, bf16[1,1,3,1024]{3,2,1,0:T(4,128)(2,1)} %get-tuple-element.11.edges), custom_call_target="tpu_custom_call" | custom-call | tf_op jit(solution)/shard_map/write_out/pallas_call | solution.py:708

commit v3 on v2

--- a/solution.py
+++ b/solution.py
@@ -63,6 +63,9 @@
     wg,
     gain,
     wout,
+    mixed_out,
+    states_out,
+    edges_out,
     mixed,
     states,
     edges,
@@ -130,6 +133,7 @@
     relay_recv,
     fl_recv,
     fr_recv,
+    out_sem,
 ):
     tok = lax.axis_index("tok")
     y = lax.axis_index("hv")
@@ -549,6 +553,13 @@
         inside = jnp.where(first + r >= pf_last, 1.0, 0.0)
         edges[0, 0, j : j + 1, :] = (ext[8 + r : 9 + r, :] * across(inside, QKV // 128)).astype(BF16)
 
+    outs = [
+        pltpu.make_async_copy(states, states_out, out_sem.at[0]),
+        pltpu.make_async_copy(edges, edges_out, out_sem.at[1]),
+    ]
+    for out in outs:
+        out.start()
+
     gated = heads(y)
     for c in (2, 3, 0, 1):
         part = project(gated, c)
@@ -557,7 +568,13 @@
         mixed[:, c * CHUNK : (c + 1) * CHUNK] = (
             part + fl[c].astype(F32) + fr[c].astype(F32)
         ).astype(BF16)
-
+        chunk = slice(c * CHUNK, (c + 1) * CHUNK)
+        out = pltpu.make_async_copy(mixed.at[:, chunk], mixed_out.at[:, chunk], out_sem.at[2 + c])
+        out.start()
+        outs.append(out)
+
+    for out in outs:
+        out.wait()
     for s in range(4):
         own_to_right(s).wait_send()
         own_to_left(s).wait_send()
@@ -578,15 +595,22 @@
         to_right(slot, fl.at[0], fl_recv.at[0]).wait_send()
 
 
-def write_out(mixed, states, edges, mixed_out, states_out, edges_out, sem):
-    copies = [
-        pltpu.make_async_copy(src, dst, sem.at[i])
-        for i, (src, dst) in enumerate([(states, states_out), (mixed, mixed_out), (edges, edges_out)])
-    ]
-    for copy in copies:
-        copy.start()
-    for copy in copies:
-        copy.wait()
+def write_out(mixed, states, edges, mixed_out, states_out, edges_out, mixed_v, states_v, edges_v, sem):
+    def copies(src, dst, i):
+        parts = [(src, dst)]
+        if src.shape[0] == DK:
+            parts = [(src.at[r : r + ROWS], dst.at[r : r + ROWS]) for r in range(0, DK, ROWS)]
+        return [pltpu.make_async_copy(a, b, sem.at[i + k]) for k, (a, b) in enumerate(parts)]
+
+    loads = copies(states, states_v, 0) + copies(mixed, mixed_v, 4) + copies(edges, edges_v, 5)
+    stores = copies(states_v, states_out, 6) + copies(mixed_v, mixed_out, 10) + copies(edges_v, edges_out, 11)
+    for load in loads:
+        load.start()
+    for load, store in zip(loads, stores):
+        load.wait()
+        store.start()
+    for store in stores:
+        store.wait()
 
 
 def shards(
@@ -608,7 +632,6 @@
     rank = decay_down.shape[1]
     dma = pltpu.SemaphoreType.DMA
     anywhere = pl.BlockSpec(memory_space=pl.ANY)
-    vmem = pl.BlockSpec(memory_space=pltpu.VMEM)
     mixed, states, edges = pl.pallas_call(
         kernel,
         out_shape=(
@@ -617,8 +640,11 @@
             jax.ShapeDtypeStruct((1, 1, 3, QKV), BF16),
         ),
         in_specs=[anywhere] * 14,
-        out_specs=(vmem, vmem, vmem),
+        out_specs=(anywhere,) * 3,
         scratch_shapes=[
+            pltpu.VMEM((ROWS, D), BF16),
+            pltpu.VMEM((DK, DV), F32),
+            pltpu.VMEM((1, 1, 3, QKV), BF16),
             pltpu.VMEM((HV, ROWS, D), BF16),
             pltpu.VMEM((D, WIDE), BF16),
             pltpu.VMEM((rank, D), BF16),
@@ -683,6 +709,7 @@
             dma((4,)),
             dma((4,)),
             dma((4,)),
+            dma((6,)),
         ],
         compiler_params=pltpu.CompilerParams(
             collective_id=0, has_side_effects=True, vmem_limit_bytes=63 * 1024 * 1024
@@ -710,7 +737,7 @@
         out_shape=tuple(jax.ShapeDtypeStruct(a.shape, a.dtype) for a in parts),
         in_specs=[anywhere] * 3,
         out_specs=(anywhere,) * 3,
-        scratch_shapes=[dma((3,))],
+        scratch_shapes=[pltpu.VMEM(a.shape, a.dtype) for a in parts] + [dma((12,))],
         name="write_out",
     )(*parts)
     return mixed, states[None, None], edges.transpose(0, 2, 1, 3)

time: 81.3 us -> 58 us (0.71)
  Pallas kernels: 80.6 us -> 57.2 us
    pallas_call x1, Pallas kernels: 25.2 us -> 2.02 us  [shards(): pl.pallas_call(write_out, out_shape=tuple((jax.ShapeDtypeStruct(a.shape,...]
where the time goes in v3:
time: 58 us; the launch traced here: 57.9 us
  Pallas kernels  57.2 us (99%)
  between operations  0.64 us (1%)
    pallas_call x1, Pallas kernels, shards(): pl.pallas_call(kernel, out_shape=(jax.ShapeDtypeStruct((ROWS, D), BF16),...  55.2 us
    pallas_call x1, Pallas kernels, shards(): pl.pallas_call(write_out, out_shape=tuple((jax.ShapeDtypeStruct(a.shape,...  2.02 us

profile of v3, /device:TPU:1, one launch (start us, length us, event | category | flops | bytes accessed | tf_op | source)
XLA Modules:
  0.0 57.9 jit_solution(11432987903767311265)
XLA Ops:
  0.6 55.2 %gla.1 = (bf16[64,2048]{1,0:T(8,128)(2,1)}, f32[256,512]{1,0:T(8,128)}, bf16[1,1,3,1024]{3,2,1,0:T(4,128)(2,1)}) custom-call(bf16[64,2048]{1,0:T(8,128)(2,1)} %tokens.1, s32[33]{0:T(128)} %lengths.1, bf16[2048,256]{1,0:T(8,128)(2,1)} %wq.1, bf16[2048,256]{1,0:T(8,128)(2,1)} %wk.1, bf16[2048,512]{1,0:T(8,128)(2,1)} %wv.1, bf16[4,256]{1,0:T(4,128)(2,1)} %cq.1, ...), custom_call_target="tpu_custom_call" | custom-call | tf_op jit(solution)/shard_map/gla/pallas_call | solution.py:635
  55.9 2.0 %write_out.1 = (bf16[64,2048]{1,0:T(8,128)(2,1)}, f32[256,512]{1,0:T(8,128)}, bf16[1,1,3,1024]{3,2,1,0:T(4,128)(2,1)}) custom-call(bf16[64,2048]{1,0:T(8,128)(2,1)} %get-tuple-element.9.mixed, f32[256,512]{1,0:T(8,128)} %get-tuple-element.10.states, bf16[1,1,3,1024]{3,2,1,0:T(4,128)(2,1)} %get-tuple-element.11.edges), custom_call_target="tpu_custom_call" | custom-call | tf_op jit(solution)/shard_map/write_out/pallas_call | solution.py:735

commit v4 on v2

--- a/solution.py
+++ b/solution.py
@@ -130,6 +130,7 @@
     relay_recv,
     fl_recv,
     fr_recv,
+    groups_in,
 ):
     tok = lax.axis_index("tok")
     y = lax.axis_index("hv")
@@ -196,8 +197,8 @@
     pl.semaphore_signal(barrier, inc=1, device_id=(before, y), device_id_type=MESH)
     for k in range(1, GROUP):
         pl.semaphore_signal(barrier, inc=1, device_id=(z * GROUP + mate(k), y), device_id_type=MESH)
-    for d in OTHERS:
-        pl.semaphore_signal(barrier, inc=1, device_id=(chip(d)[1], y), device_id_type=MESH)
+    for k in range(1, PLANES):
+        pl.semaphore_signal(barrier, inc=1, device_id=(peer(k) * GROUP + g, y), device_id_type=MESH)
     for copy in small[:2]:
         copy.start()
     for c in range(D // CHUNK):
@@ -205,7 +206,7 @@
             copy.start()
     for copy in small[2:]:
         copy.start()
-    pl.semaphore_wait(barrier, 4 + GROUP - 1 + len(OTHERS))
+    pl.semaphore_wait(barrier, 4 + GROUP - 1 + PLANES - 1)
 
     def cols(c):
         return pl.ds(pl.multiple_of(c * CHUNK, CHUNK), CHUNK)
@@ -248,6 +249,9 @@
     for s in range(4):
         own_to_right(s).start()
         own_to_left(s).start()
+
+    for k in range(1, PLANES):
+        pl.semaphore_signal(groups_in, inc=1, device_id=(peer(k) * GROUP + g, y), device_id_type=MESH)
 
     acc[...] = jnp.zeros_like(acc)
     accl[...] = jnp.zeros_like(accl)
@@ -420,6 +424,7 @@
         k, device = chip(d)
         return remote(dst.at[k], dst.at[k], ss.at[0], rs.at[k], device, y)
 
+    pl.semaphore_wait(groups_in, PLANES - 1)
     for i, d in enumerate(OTHERS):
         to_chip(i, d, ts, tr, t_send, t_recv).start()
     tr[me] = ts[me]
@@ -579,14 +584,18 @@
 
 
 def write_out(mixed, states, edges, mixed_out, states_out, edges_out, sem):
-    copies = [
-        pltpu.make_async_copy(src, dst, sem.at[i])
-        for i, (src, dst) in enumerate([(states, states_out), (mixed, mixed_out), (edges, edges_out)])
-    ]
-    for copy in copies:
-        copy.start()
-    for copy in copies:
-        copy.wait()
+    def copies(src, dst, i, step):
+        rows = src.shape[0]
+        return [
+            pltpu.make_async_copy(src.at[r : r + step], dst.at[r : r + step], sem.at[i + r // step])
+            for r in range(0, rows, step)
+        ]
+
+    stores = copies(states, states_out, 0, ROWS) + copies(mixed, mixed_out, 4, 32) + copies(edges, edges_out, 6, 1)
+    for store in stores:
+        store.start()
+    for store in stores:
+        store.wait()
 
 
 def shards(
@@ -612,9 +621,9 @@
     mixed, states, edges = pl.pallas_call(
         kernel,
         out_shape=(
-            jax.ShapeDtypeStruct((ROWS, D), BF16),
-            jax.ShapeDtypeStruct((DK, DV), F32),
-            jax.ShapeDtypeStruct((1, 1, 3, QKV), BF16),
+            pltpu.VMEM((ROWS, D), BF16),
+            pltpu.VMEM((DK, DV), F32),
+            pltpu.VMEM((1, 1, 3, QKV), BF16),
         ),
         in_specs=[anywhere] * 14,
         out_specs=(vmem, vmem, vmem),
@@ -683,36 +692,42 @@
             dma((4,)),
             dma((4,)),
             dma((4,)),
+            pltpu.SemaphoreType.REGULAR,
         ],
         compiler_params=pltpu.CompilerParams(
-            collective_id=0, has_side_effects=True, vmem_limit_bytes=63 * 1024 * 1024
+            collective_id=0, has_side_effects=True, vmem_limit_bytes=48 * 1024 * 1024
         ),
         name="gla",
     )(
-        tokens,
-        prompt_lengths,
-        query_weight,
-        key_weight,
-        value_weight,
-        query_conv,
-        key_conv,
-        value_conv,
-        decay_down.T,
-        decay_up,
-        decay_bias.reshape(1, DK),
-        gate_weight,
-        norm_gain.reshape(1, DV),
-        out_weight,
+        *[
+            pltpu.with_memory_space_constraint(a, pltpu.HBM)
+            for a in (
+                tokens,
+                prompt_lengths,
+                query_weight,
+                key_weight,
+                value_weight,
+                query_conv,
+                key_conv,
+                value_conv,
+                decay_down.T,
+                decay_up,
+                decay_bias.reshape(1, DK),
+                gate_weight,
+                norm_gain.reshape(1, DV),
+                out_weight,
+            )
+        ]
     )
     parts = (mixed, states, edges)
     mixed, states, edges = pl.pallas_call(
         write_out,
         out_shape=tuple(jax.ShapeDtypeStruct(a.shape, a.dtype) for a in parts),
-        in_specs=[anywhere] * 3,
+        in_specs=[vmem] * 3,
         out_specs=(anywhere,) * 3,
-        scratch_shapes=[dma((3,))],
+        scratch_shapes=[dma((7,))],
         name="write_out",
-    )(*parts)
+    )(*[pltpu.with_memory_space_constraint(a, pltpu.VMEM) for a in parts])
     return mixed, states[None, None], edges.transpose(0, 2, 1, 3)
 
 

time: 81.3 us -> 55.1 us (0.68)
  Pallas kernels: 80.6 us -> 54.4 us
    pallas_call x1, Pallas kernels: 25.2 us -> 0.94 us  [shards(): pl.pallas_call(write_out, out_shape=tuple((jax.ShapeDtypeStruct(a.shape,...]
    pallas_call x1, Pallas kernels: 55.4 us -> 53.5 us  [shards(): pl.pallas_call(kernel, out_shape=(pltpu.VMEM((ROWS, D), BF16), pltpu.VMEM...]
where the time goes in v4:
time: 55.1 us; the launch traced here: 55 us
  Pallas kernels  54.4 us (99%)
  between operations  0.64 us (1%)
    pallas_call x1, Pallas kernels, shards(): pl.pallas_call(kernel, out_shape=(pltpu.VMEM((ROWS, D), BF16), pltpu.VMEM...  53.5 us

profile of v4, /device:TPU:1, one launch (start us, length us, event | category | flops | bytes accessed | tf_op | source)
XLA Modules:
  0.0 55.0 jit_solution(3069083617074771537)
XLA Ops:
  0.6 53.5 %gla.1 = (bf16[64,2048]{1,0:T(8,128)(2,1)S(1)}, f32[256,512]{1,0:T(8,128)S(1)}, bf16[1,1,3,1024]{3,2,1,0:T(4,128)(2,1)S(1)}) custom-call(bf16[64,2048]{1,0:T(8,128)(2,1)} %tokens.1, s32[33]{0:T(128)} %lengths.1, bf16[2048,256]{1,0:T(8,128)(2,1)} %wq.1, bf16[2048,256]{1,0:T(8,128)(2,1)} %wk.1, bf16[2048,512]{1,0:T(8,128)(2,1)} %wv.1, bf16[4,256]{1,0:T(4,128)(2,1)} %cq.1, ...), custom_call_target="tpu_custom_call" | custom-call | tf_op jit(solution)/shard_map/gla/pallas_call | solution.py:621
  54.1 0.9 %write_out.1 = (bf16[64,2048]{1,0:T(8,128)(2,1)}, f32[256,512]{1,0:T(8,128)}, bf16[1,1,3,1024]{3,2,1,0:T(4,128)(2,1)}) custom-call(bf16[64,2048]{1,0:T(8,128)(2,1)S(1)} %get-tuple-element.9.mixed, f32[256,512]{1,0:T(8,128)S(1)} %get-tuple-element.10.states, bf16[1,1,3,1024]{3,2,1,0:T(4,128)(2,1)S(1)} %get-tuple-element.11.edges), custom_call_target="tpu_custom_call" | custom-call | tf_op jit(solution)/shard_map/write_out/pallas_call | solution.py:723

commit v5 on v4

--- a/solution.py
+++ b/solution.py
@@ -109,8 +109,7 @@
     er,
     rs_s,
     relay,
-    fl,
-    fr,
+    fin,
     w_sem,
     loc_sem,
     tk_send,
@@ -128,8 +127,7 @@
     pe_sem,
     rs_send,
     relay_recv,
-    fl_recv,
-    fr_recv,
+    f_recv,
     groups_in,
 ):
     tok = lax.axis_index("tok")
@@ -151,6 +149,10 @@
             src_ref=src, dst_ref=dst, send_sem=ss, recv_sem=rs, device_id=(to_tok, to_hv), device_id_type=MESH
         )
 
+    def batch(ref, n, ss, rs):
+        part = ref.at[pl.ds(0, n)]
+        return remote(part, part, ss, rs, sib, y)
+
     def mate(k):
         return lax.rem(g + k, GROUP)
 
@@ -167,10 +169,10 @@
     def weight_copies(c):
         rows = pl.ds(c * CHUNK, CHUNK)
         return [
-            pltpu.make_async_copy(wq.at[rows], wall.at[rows, 0:DK], w_sem.at[c, 0]),
-            pltpu.make_async_copy(wk.at[rows], wall.at[rows, DK : 2 * DK], w_sem.at[c, 1]),
-            pltpu.make_async_copy(wv.at[rows], wall.at[rows, 2 * DK : QKV], w_sem.at[c, 2]),
-            pltpu.make_async_copy(wg.at[rows], wall.at[rows, QKV:WIDE], w_sem.at[c, 3]),
+            pltpu.make_async_copy(wq.at[rows], wall.at[rows, 0:DK], w_sem.at[c]),
+            pltpu.make_async_copy(wk.at[rows], wall.at[rows, DK : 2 * DK], w_sem.at[c]),
+            pltpu.make_async_copy(wv.at[rows], wall.at[rows, 2 * DK : QKV], w_sem.at[c]),
+            pltpu.make_async_copy(wg.at[rows], wall.at[rows, QKV:WIDE], w_sem.at[c]),
         ]
 
     small = [
@@ -213,38 +215,38 @@
 
     def own_to_right(s):
         return remote(
-            tokens.at[:, cols(s)], xt.at[y, :, cols(s)], tk_send.at[0, s], tk_recv.at[0, s], tok, right
+            tokens.at[:, cols(s)], xt.at[y, :, cols(s)], tk_send.at[0], tk_recv.at[0, s], tok, right
         )
 
     def own_to_left(s):
         c = lax.rem(s + 2, 4)
         return remote(
-            tokens.at[:, cols(c)], xt.at[y, :, cols(c)], tk_send.at[1, s], tk_recv.at[1, s], tok, left
+            tokens.at[:, cols(c)], xt.at[y, :, cols(c)], tk_send.at[0], tk_recv.at[1, s], tok, left
         )
 
     def from_left(s):
         part = xt.at[left, :, cols(s)]
-        return remote(part, part, tk_send.at[0, s], tk_recv.at[0, s], tok, right)
+        return remote(part, part, tk_send.at[0], tk_recv.at[0, s], tok, right)
 
     def from_right(s):
         part = xt.at[right, :, cols(lax.rem(s + 2, 4))]
-        return remote(part, part, tk_send.at[1, s], tk_recv.at[1, s], tok, left)
+        return remote(part, part, tk_send.at[0], tk_recv.at[1, s], tok, left)
 
     def on_to_right(f):
         part = xt.at[left, :, cols(f)]
-        return remote(part, part, tk_send.at[0, 4 + f], tk_recv.at[0, 4 + f], tok, right)
+        return remote(part, part, tk_send.at[0], tk_recv.at[0, 4 + f], tok, right)
 
     def on_to_left(f):
         part = xt.at[right, :, cols(f + 2)]
-        return remote(part, part, tk_send.at[1, 4 + f], tk_recv.at[1, 4 + f], tok, left)
+        return remote(part, part, tk_send.at[0], tk_recv.at[1, 4 + f], tok, left)
 
     def far_from_left(f):
         part = xt.at[opp, :, cols(f)]
-        return remote(part, part, tk_send.at[0, 4 + f], tk_recv.at[0, 4 + f], tok, right)
+        return remote(part, part, tk_send.at[0], tk_recv.at[0, 4 + f], tok, right)
 
     def far_from_right(f):
         part = xt.at[opp, :, cols(f + 2)]
-        return remote(part, part, tk_send.at[1, 4 + f], tk_recv.at[1, 4 + f], tok, left)
+        return remote(part, part, tk_send.at[0], tk_recv.at[1, 4 + f], tok, left)
 
     for s in range(4):
         own_to_right(s).start()
@@ -288,8 +290,8 @@
     own.wait()
 
     def own_step(c, _):
-        for copy in weight_copies(c):
-            copy.wait()
+        part = wall.at[pl.ds(c * CHUNK, CHUNK)]
+        pltpu.make_async_copy(part, part, w_sem.at[c]).wait()
         gemm(y, c)
         return 0
 
@@ -346,11 +348,11 @@
     pf_last = pf_col[SEG - 1 : SEG, :]
     whole = jnp.where(pf_last < first, 1.0, 0.0)
     dsend[...] = jnp.broadcast_to(jnp.exp(c_last) * across(whole, DK // 128), (8, DK))
-    remote(dsend, dgat.at[g], d_send.at[0], d_recv.at[g], sib, y).start()
+    remote(dsend, dgat.at[g], d_send.at[0], d_recv.at[0], sib, y).start()
     for dx in (2, 1, 3):
         for dc in range(2):
             to = z * GROUP + lax.rem(x + dx, XS) * 2 + lax.rem(core + dc, 2)
-            remote(dsend, dgat.at[g], d_send.at[2 * dx + dc], d_recv.at[g], to, y).start()
+            remote(dsend, dgat.at[g], d_send.at[0], d_recv.at[1], to, y).start()
     dgat[g] = dsend[...]
 
     def conv(r0, n, source, base, c0, width, taps, t0):
@@ -362,14 +364,14 @@
         half = 0.5 * total
         return (half * jnp.tanh(half) + half).astype(BF16)
 
-    def conv_all(c0, width, taps, store):
+    def conv_all(c0, width, taps, store, t_from=0):
         for r0 in [8, 16] + list(range(32, SEG, 32)):
             n = 8 if r0 == 8 else 16 if r0 == 16 else 32
-            for t0 in range(0, width, 256):
+            for t0 in range(t_from, width, 256):
                 store(r0, n, t0, conv(r0, n, ext, 8, c0 + t0, 256, taps, t0))
 
-    def conv_first(c0, width, taps, store):
-        for t0 in range(0, width, 256):
+    def conv_first(c0, width, taps, store, t_from=0):
+        for t0 in range(t_from, width, 256):
             store(0, 8, t0, conv(0, 8, ext, 8, c0 + t0, 256, taps, t0))
 
     def store_k(r0, n, t0, value):
@@ -379,25 +381,32 @@
         convv[r0 : r0 + n, t0 : t0 + 256] = value.astype(F32)
 
     conv_all(DK, DK, taps_k, store_k)
-    conv_all(2 * DK, DV, taps_v, store_v)
+    conv_all(2 * DK, DV // 2, taps_v, store_v)
 
     remote(ext.at[SEG : SEG + 8], halo, halo_sem.at[0], halo_sem.at[1], after, y).wait_recv()
     ext[0:8, :] = halo[...]
     conv_first(DK, DK, taps_k, store_k)
-    conv_first(2 * DK, DV, taps_v, store_v)
+    conv_first(2 * DK, DV // 2, taps_v, store_v)
 
     tail = jnp.where(pf_col[...] == pf_last, 1.0, 0.0)
     weighted = (convk[...] * jnp.exp(c_last - cum[...]) * across(tail, DK // 128)).astype(BF16)
-    local[...] = dot_tn(weighted, convv[...].astype(BF16))
 
     def half_rows(which):
         return pl.ds(pl.multiple_of(which * HALF, HALF), HALF)
 
-    pair_s[...] = local[half_rows(1 - core), :].astype(BF16)
-    to_sib = remote(pair_s, pair_r, pair_sem.at[0], pair_sem.at[1], sib, y)
-    to_sib.start()
+    def part_cols(p):
+        return slice(p * (DV // 2), (p + 1) * (DV // 2))
+
+    to_sib = [remote(pair_s.at[p], pair_r.at[p], pair_sem.at[0, p], pair_sem.at[1, p], sib, y) for p in range(2)]
+    for p in range(2):
+        if p == 1:
+            conv_all(2 * DK, DV, taps_v, store_v, DV // 2)
+            conv_first(2 * DK, DV, taps_v, store_v, DV // 2)
+        local[:, part_cols(p)] = dot_tn(weighted, convv[:, part_cols(p)].astype(BF16))
+        pair_s[p] = local[half_rows(1 - core), part_cols(p)].astype(BF16)
+        to_sib[p].start()
     sib_g = g + 1 - 2 * core
-    remote(dsend, dgat.at[sib_g], d_send.at[0], d_recv.at[sib_g], sib, y).wait_recv()
+    remote(dsend, dgat.at[sib_g], d_send.at[0], d_recv.at[0], sib, y).wait_recv()
     dmat[0:8, :] = dsend[...]
     dmat[8:16, :] = dgat[sib_g]
     dts[...] = jnp.transpose(dmat[...])
@@ -406,33 +415,42 @@
     is_first = core == 0
     d_first = jnp.where(is_first, own_d, sib_d)
     d_second = jnp.where(is_first, sib_d, own_d)
-    to_sib.wait_recv()
-    own_l = local[half_rows(core), :]
-    sib_l = pair_r[...].astype(F32)
-    l_first = jnp.where(is_first, own_l, sib_l)
-    first_l[...] = l_first
-    chip_l = (l_first * d_second + jnp.where(is_first, sib_l, own_l)).astype(BF16)
-    for k in range(CHIPS):
-        ts[k] = chip_l[16 * (k // XS) : 16 * (k // XS) + 16, 128 * (k % XS) : 128 * (k % XS) + 128]
     me = z * XS + x
 
-    def to_chip(i, d, src, dst, ss, rs):
+    def to_chip(d, src, dst, ss, rs):
         k, device = chip(d)
-        return remote(src.at[k], dst.at[me], ss.at[i], rs.at[me], device, y)
-
-    def from_chip(d, dst, ss, rs):
-        k, device = chip(d)
-        return remote(dst.at[k], dst.at[k], ss.at[0], rs.at[k], device, y)
+        return remote(src.at[k], dst.at[me], ss.at[0], rs.at[0], device, y)
+
+    def tile_to(dz, to_x):
+        to_z = lax.rem(z + dz, PLANES)
+        k = to_z * XS + to_x
+        return remote(ts.at[k], tr.at[me], t_send.at[0], t_recv.at[0], to_z * GROUP + to_x * 2 + core, y)
+
+    def send_tiles(to_xs):
+        for dz in (4, 3, 5, 2, 6, 1, 7):
+            for to_x in to_xs:
+                tile_to(dz, to_x).start()
+        for to_x in to_xs:
+
+            @pl.when(x != to_x)
+            def _():
+                tile_to(0, to_x).start()
 
     pl.semaphore_wait(groups_in, PLANES - 1)
-    for i, d in enumerate(OTHERS):
-        to_chip(i, d, ts, tr, t_send, t_recv).start()
+    for p in range(2):
+        to_sib[p].wait_recv()
+        own_l = local[half_rows(core), part_cols(p)]
+        sib_l = pair_r[p].astype(F32)
+        l_first = jnp.where(is_first, own_l, sib_l)
+        first_l[:, part_cols(p)] = l_first
+        chip_l = (l_first * d_second + jnp.where(is_first, sib_l, own_l)).astype(BF16)
+        for to_z in range(PLANES):
+            for i in range(2):
+                ts[to_z * XS + 2 * p + i] = chip_l[16 * to_z : 16 * to_z + 16, 128 * i : 128 * i + 128]
+        send_tiles((2 * p, 2 * p + 1))
     tr[me] = ts[me]
 
-    for dx in (1, 3, 2):
-        for dc in range(2):
-            j = lax.rem(x + dx, XS) * 2 + lax.rem(core + dc, 2)
-            remote(dsend, dgat.at[j], d_send.at[0], d_recv.at[j], z * GROUP + j, y).wait_recv()
+    batch(dgat, GROUP - 2, d_send.at[0], d_recv.at[1]).wait_recv()
 
     sub = lax.broadcasted_iota(jnp.int32, (8, HALF), 0)
     chips_d = jnp.zeros((8, HALF), F32)
@@ -441,7 +459,7 @@
         chips_d = jnp.where(sub == j, jnp.where(is_first, both[:, 0:HALF], both[:, HALF:DK]), chips_d)
     gsend[...] = chips_d
     for k in (4, 3, 5, 2, 6, 1, 7):
-        remote(gsend, ggat.at[z], g_send.at[k], g_recv.at[z], peer(k) * GROUP + g, y).start()
+        remote(gsend, ggat.at[z], g_send.at[0], g_recv.at[0], peer(k) * GROUP + g, y).start()
     ggat[z] = gsend[...]
 
     def store_q(r0, n, t0, value):
@@ -470,22 +488,19 @@
         scores = jnp.where((ri >= ci) & same, scores, 0.0).astype(BF16)
         inner[r0:r1, :] = dot(scores, convv[0:r1, :].astype(BF16))
 
-    for k in range(1, PLANES):
-        j = peer(k)
-        remote(gsend, ggat.at[j], g_send.at[k], g_recv.at[j], j * GROUP + g, y).wait_recv()
+    batch(ggat, PLANES - 1, g_send.at[0], g_recv.at[0]).wait_recv()
     padded = jnp.concatenate([ggat[...].reshape(8 * PLANES, HALF), jnp.zeros((64, HALF), F32)], axis=0)
     dt[...] = jnp.transpose(padded)
 
-    for d in OTHERS:
-        from_chip(d, tr, t_send, t_recv).wait_recv()
+    batch(tr, CHIPS - 1, t_send.at[0], t_recv.at[0]).wait_recv()
     tile_d = dt[pl.ds(pl.multiple_of(16 * z, 16), 16), :]
     run = jnp.zeros((16, 128), F32)
     for k in range(CHIPS):
         qs[k] = run.astype(BF16)
         lane = 8 * (k // XS) + k % XS
         run = run * tile_d[:, lane : lane + 1] + tr[k].astype(F32)
-    for i, d in enumerate(OTHERS):
-        to_chip(i, d, qs, qr, q_send, q_recv).start()
+    for d in OTHERS:
+        to_chip(d, qs, qr, q_send, q_recv).start()
     qr[me] = qs[me]
 
     for b in range(SEG // ROWS):
@@ -493,8 +508,7 @@
         half = 0.5 * gate
         gg[b] = (half * jnp.tanh(half) + half) * gain_v[...]
 
-    for d in OTHERS:
-        from_chip(d, qr, q_send, q_recv).wait_recv()
+    batch(qr, CHIPS - 1, q_send.at[0], q_recv.at[0]).wait_recv()
     at_first = jnp.concatenate(
         [jnp.concatenate([qr[XS * a + b].astype(F32) for b in range(XS)], axis=1) for a in range(PLANES)],
         axis=0,
@@ -518,10 +532,10 @@
         return dot(gated, wo[:, c * CHUNK : (c + 1) * CHUNK])
 
     def to_right(slot, dst, sem):
-        return remote(rs_s.at[slot], dst, rs_send.at[slot], sem, tok, right)
+        return remote(rs_s.at[slot], dst, rs_send.at[0], sem, tok, right)
 
     def to_left(slot, dst, sem):
-        return remote(rs_s.at[slot], dst, rs_send.at[slot], sem, tok, left)
+        return remote(rs_s.at[slot], dst, rs_send.at[0], sem, tok, left)
 
     gated = heads(opp)
     for c in (0, 2, 1, 3):
@@ -532,21 +546,21 @@
     for i in range(2):
         c = 2 + i
         rs_s[4 + c] = project(gated_r, c).astype(BF16)
-        to_right(4 + c, fl.at[c], fl_recv.at[c]).start()
+        to_right(4 + c, fin.at[c, 0], f_recv.at[c]).start()
         c = i
         rs_s[4 + c] = project(gated_l, c).astype(BF16)
-        to_left(4 + c, fr.at[c], fr_recv.at[c]).start()
+        to_left(4 + c, fin.at[c, 1], f_recv.at[c]).start()
     for i in range(2):
         c = i
         part = project(gated_r, c)
         to_right(c, relay.at[c], relay_recv.at[c]).wait_recv()
         rs_s[8 + c] = (part + relay[c].astype(F32)).astype(BF16)
-        to_right(8 + c, fl.at[c], fl_recv.at[c]).start()
+        to_right(8 + c, fin.at[c, 0], f_recv.at[c]).start()
         c = 2 + i
         part = project(gated_l, c)
         to_left(c, relay.at[c], relay_recv.at[c]).wait_recv()
         rs_s[8 + c] = (part + relay[c].astype(F32)).astype(BF16)
-        to_left(8 + c, fr.at[c], fr_recv.at[c]).start()
+        to_left(8 + c, fin.at[c, 1], f_recv.at[c]).start()
 
     states[...] = er[...].reshape(DK, DV).astype(F32) * dts[:, 0:1] + local[...]
     for j in range(3):
@@ -557,30 +571,21 @@
     gated = heads(y)
     for c in (2, 3, 0, 1):
         part = project(gated, c)
-        to_right(0, fl.at[c], fl_recv.at[c]).wait_recv()
-        to_right(0, fr.at[c], fr_recv.at[c]).wait_recv()
+        remote(fin.at[c], fin.at[c], rs_send.at[0], f_recv.at[c], tok, right).wait_recv()
         mixed[:, c * CHUNK : (c + 1) * CHUNK] = (
-            part + fl[c].astype(F32) + fr[c].astype(F32)
+            part + fin[c, 0].astype(F32) + fin[c, 1].astype(F32)
         ).astype(BF16)
 
-    for s in range(4):
-        own_to_right(s).wait_send()
-        own_to_left(s).wait_send()
-    for f in range(2):
-        on_to_right(f).wait_send()
-        on_to_left(f).wait_send()
+    batch(xt, HV - 1, tk_send.at[0], tk_recv.at[0, 0]).wait_send()
     halo_copy.wait_send()
-    for k in [0] + list(range(2, 8)):
-        remote(dsend, dgat.at[g], d_send.at[k], d_recv.at[g], sib, y).wait_send()
-    for k in range(1, PLANES):
-        remote(gsend, ggat.at[z], g_send.at[k], g_recv.at[z], sib, y).wait_send()
-    to_sib.wait_send()
+    batch(dgat, GROUP - 1, d_send.at[0], d_recv.at[0]).wait_send()
+    batch(ggat, PLANES - 1, g_send.at[0], g_recv.at[0]).wait_send()
+    for copy in to_sib:
+        copy.wait_send()
+    batch(ts, CHIPS - 1, t_send.at[0], t_recv.at[0]).wait_send()
     sib_e.wait_send()
-    for i, d in enumerate(OTHERS):
-        to_chip(i, d, ts, tr, t_send, t_recv).wait_send()
-        to_chip(i, d, qs, qr, q_send, q_recv).wait_send()
-    for slot in range(12):
-        to_right(slot, fl.at[0], fl_recv.at[0]).wait_send()
+    batch(qs, CHIPS - 1, q_send.at[0], q_recv.at[0]).wait_send()
+    batch(rs_s, 12, rs_send.at[0], f_recv.at[0]).wait_send()
 
 
 def write_out(mixed, states, edges, mixed_out, states_out, edges_out, sem):
@@ -660,8 +665,8 @@
             pltpu.VMEM((128, DK), F32),
             pltpu.VMEM((DK, 128), F32),
             pltpu.VMEM((HALF, 128), F32),
-            pltpu.VMEM((HALF, DV), BF16),
-            pltpu.VMEM((HALF, DV), BF16),
+            pltpu.VMEM((2, HALF, DV // 2), BF16),
+            pltpu.VMEM((2, HALF, DV // 2), BF16),
             pltpu.VMEM((HALF, DV), F32),
             pltpu.VMEM((CHIPS, 16, 128), BF16),
             pltpu.VMEM((CHIPS, 16, 128), BF16),
@@ -671,25 +676,23 @@
             pltpu.VMEM((2, HALF, DV), BF16),
             pltpu.VMEM((12, ROWS, CHUNK), BF16),
             pltpu.VMEM((4, ROWS, CHUNK), BF16),
-            pltpu.VMEM((4, ROWS, CHUNK), BF16),
-            pltpu.VMEM((4, ROWS, CHUNK), BF16),
-            dma((4, 4)),
+            pltpu.VMEM((4, 2, ROWS, CHUNK), BF16),
+            dma((4,)),
             dma((10,)),
-            dma((2, 6)),
+            dma((1,)),
             dma((2, 6)),
             dma((2,)),
-            dma((8,)),
-            dma((8,)),
-            dma((8,)),
-            dma((8,)),
+            dma((1,)),
             dma((2,)),
-            dma((CHIPS,)),
-            dma((CHIPS,)),
-            dma((CHIPS,)),
-            dma((CHIPS,)),
+            dma((1,)),
+            dma((1,)),
+            dma((2, 2)),
+            dma((1,)),
+            dma((1,)),
+            dma((1,)),
+            dma((1,)),
             dma((2,)),
-            dma((12,)),
-            dma((4,)),
+            dma((1,)),
             dma((4,)),
             dma((4,)),
             pltpu.SemaphoreType.REGULAR,

time: 55.1 us -> 53.1 us (0.964)
  Pallas kernels: 54.4 us -> 52.3 us
    pallas_call x1, Pallas kernels: 53.5 us -> 51.4 us  [shards(): pl.pallas_call(kernel, out_shape=(pltpu.VMEM((ROWS, D), BF16), pltpu.VMEM...]
where the time goes in v5:
time: 53.1 us; the launch traced here: 53 us
  Pallas kernels  52.3 us (98%)
  between operations  0.64 us (1%)
    pallas_call x1, Pallas kernels, shards(): pl.pallas_call(kernel, out_shape=(pltpu.VMEM((ROWS, D), BF16), pltpu.VMEM...  51.4 us

profile of v5, /device:TPU:1, one launch (start us, length us, event | category | flops | bytes accessed | tf_op | source)
XLA Modules:
  0.0 53.0 jit_solution(17161246760732086507)
XLA Ops:
  0.6 51.4 %gla.1 = (bf16[64,2048]{1,0:T(8,128)(2,1)S(1)}, f32[256,512]{1,0:T(8,128)S(1)}, bf16[1,1,3,1024]{3,2,1,0:T(4,128)(2,1)S(1)}) custom-call(bf16[64,2048]{1,0:T(8,128)(2,1)} %tokens.1, s32[33]{0:T(128)} %lengths.1, bf16[2048,256]{1,0:T(8,128)(2,1)} %wq.1, bf16[2048,256]{1,0:T(8,128)(2,1)} %wk.1, bf16[2048,512]{1,0:T(8,128)(2,1)} %wv.1, bf16[4,256]{1,0:T(4,128)(2,1)} %cq.1, ...), custom_call_target="tpu_custom_call" | custom-call | tf_op jit(solution)/shard_map/gla/pallas_call | solution.py:626
  52.1 0.9 %write_out.1 = (bf16[64,2048]{1,0:T(8,128)(2,1)}, f32[256,512]{1,0:T(8,128)}, bf16[1,1,3,1024]{3,2,1,0:T(4,128)(2,1)}) custom-call(bf16[64,2048]{1,0:T(8,128)(2,1)S(1)} %get-tuple-element.9.mixed, f32[256,512]{1,0:T(8,128)S(1)} %get-tuple-element.10.states, bf16[1,1,3,1024]{3,2,1,0:T(4,128)(2,1)S(1)} %get-tuple-element.11.edges), custom_call_target="tpu_custom_call" | custom-call | tf_op jit(solution)/shard_map/write_out/pallas_call | solution.py:726

commit v6 on v5

--- a/solution.py
+++ b/solution.py
@@ -164,7 +164,6 @@
         return other_z * XS + other_x, other_z * GROUP + other_x * 2 + core
 
     own = pltpu.make_async_copy(tokens, xt.at[y], loc_sem.at[0])
-    own.start()
 
     def weight_copies(c):
         rows = pl.ds(c * CHUNK, CHUNK)
@@ -201,6 +200,50 @@
         pl.semaphore_signal(barrier, inc=1, device_id=(z * GROUP + mate(k), y), device_id_type=MESH)
     for k in range(1, PLANES):
         pl.semaphore_signal(barrier, inc=1, device_id=(peer(k) * GROUP + g, y), device_id_type=MESH)
+    pl.semaphore_wait(barrier, 4 + GROUP - 1 + PLANES - 1)
+
+    def cols(c):
+        return pl.ds(pl.multiple_of(c * CHUNK, CHUNK), CHUNK)
+
+    def own_to_right(s):
+        return remote(
+            tokens.at[:, cols(s)], xt.at[y, :, cols(s)], tk_send.at[0], tk_recv.at[0, s], tok, right
+        )
+
+    def own_to_left(s):
+        c = lax.rem(s + 2, 4)
+        return remote(
+            tokens.at[:, cols(c)], xt.at[y, :, cols(c)], tk_send.at[0], tk_recv.at[1, s], tok, left
+        )
+
+    def from_left(s):
+        part = xt.at[left, :, cols(s)]
+        return remote(part, part, tk_send.at[0], tk_recv.at[0, s], tok, right)
+
+    def from_right(s):
+        part = xt.at[right, :, cols(lax.rem(s + 2, 4))]
+        return remote(part, part, tk_send.at[0], tk_recv.at[1, s], tok, left)
+
+    def on_to_right(f):
+        part = xt.at[left, :, cols(f)]
+        return remote(part, part, tk_send.at[0], tk_recv.at[0, 4 + f], tok, right)
+
+    def on_to_left(f):
+        part = xt.at[right, :, cols(f + 2)]
+        return remote(part, part, tk_send.at[0], tk_recv.at[1, 4 + f], tok, left)
+
+    def far_from_left(f):
+        part = xt.at[opp, :, cols(f)]
+        return remote(part, part, tk_send.at[0], tk_recv.at[0, 4 + f], tok, right)
+
+    def far_from_right(f):
+        part = xt.at[opp, :, cols(f + 2)]
+        return remote(part, part, tk_send.at[0], tk_recv.at[1, 4 + f], tok, left)
+
+    for s in range(4):
+        own_to_right(s).start()
+        own_to_left(s).start()
+    own.start()
     for copy in small[:2]:
         copy.start()
     for c in range(D // CHUNK):
@@ -208,49 +251,6 @@
             copy.start()
     for copy in small[2:]:
         copy.start()
-    pl.semaphore_wait(barrier, 4 + GROUP - 1 + PLANES - 1)
-
-    def cols(c):
-        return pl.ds(pl.multiple_of(c * CHUNK, CHUNK), CHUNK)
-
-    def own_to_right(s):
-        return remote(
-            tokens.at[:, cols(s)], xt.at[y, :, cols(s)], tk_send.at[0], tk_recv.at[0, s], tok, right
-        )
-
-    def own_to_left(s):
-        c = lax.rem(s + 2, 4)
-        return remote(
-            tokens.at[:, cols(c)], xt.at[y, :, cols(c)], tk_send.at[0], tk_recv.at[1, s], tok, left
-        )
-
-    def from_left(s):
-        part = xt.at[left, :, cols(s)]
-        return remote(part, part, tk_send.at[0], tk_recv.at[0, s], tok, right)
-
-    def from_right(s):
-        part = xt.at[right, :, cols(lax.rem(s + 2, 4))]
-        return remote(part, part, tk_send.at[0], tk_recv.at[1, s], tok, left)
-
-    def on_to_right(f):
-        part = xt.at[left, :, cols(f)]
-        return remote(part, part, tk_send.at[0], tk_recv.at[0, 4 + f], tok, right)
-
-    def on_to_left(f):
-        part = xt.at[right, :, cols(f + 2)]
-        return remote(part, part, tk_send.at[0], tk_recv.at[1, 4 + f], tok, left)
-
-    def far_from_left(f):
-        part = xt.at[opp, :, cols(f)]
-        return remote(part, part, tk_send.at[0], tk_recv.at[0, 4 + f], tok, right)
-
-    def far_from_right(f):
-        part = xt.at[opp, :, cols(f + 2)]
-        return remote(part, part, tk_send.at[0], tk_recv.at[1, 4 + f], tok, left)
-
-    for s in range(4):
-        own_to_right(s).start()
-        own_to_left(s).start()
 
     for k in range(1, PLANES):
         pl.semaphore_signal(groups_in, inc=1, device_id=(peer(k) * GROUP + g, y), device_id_type=MESH)
@@ -389,7 +389,7 @@
     conv_first(2 * DK, DV // 2, taps_v, store_v)
 
     tail = jnp.where(pf_col[...] == pf_last, 1.0, 0.0)
-    weighted = (convk[...] * jnp.exp(c_last - cum[...]) * across(tail, DK // 128)).astype(BF16)
+    weighted = jnp.transpose(convk[...] * jnp.exp(c_last - cum[...]) * across(tail, DK // 128)).astype(BF16)
 
     def half_rows(which):
         return pl.ds(pl.multiple_of(which * HALF, HALF), HALF)
@@ -402,7 +402,7 @@
         if p == 1:
             conv_all(2 * DK, DV, taps_v, store_v, DV // 2)
             conv_first(2 * DK, DV, taps_v, store_v, DV // 2)
-        local[:, part_cols(p)] = dot_tn(weighted, convv[:, part_cols(p)].astype(BF16))
+        local[:, part_cols(p)] = dot(weighted, convv[:, part_cols(p)].astype(BF16))
         pair_s[p] = local[half_rows(1 - core), part_cols(p)].astype(BF16)
         to_sib[p].start()
     sib_g = g + 1 - 2 * core

time: 53.1 us -> 53.1 us (level)
  no operation moved by 1% of the time
where the time goes in v6:
time: 53.1 us; the launch traced here: 53 us
  Pallas kernels  52.3 us (98%)
  between operations  0.64 us (1%)
    pallas_call x1, Pallas kernels, shards(): pl.pallas_call(kernel, out_shape=(pltpu.VMEM((ROWS, D), BF16), pltpu.VMEM...  51.4 us

profile of v6, /device:TPU:1, one launch (start us, length us, event | category | flops | bytes accessed | tf_op | source)
XLA Modules:
  0.0 53.0 jit_solution(11443761655709307372)
XLA Ops:
  0.6 51.4 %gla.1 = (bf16[64,2048]{1,0:T(8,128)(2,1)S(1)}, f32[256,512]{1,0:T(8,128)S(1)}, bf16[1,1,3,1024]{3,2,1,0:T(4,128)(2,1)S(1)}) custom-call(bf16[64,2048]{1,0:T(8,128)(2,1)} %tokens.1, s32[33]{0:T(128)} %lengths.1, bf16[2048,256]{1,0:T(8,128)(2,1)} %wq.1, bf16[2048,256]{1,0:T(8,128)(2,1)} %wk.1, bf16[2048,512]{1,0:T(8,128)(2,1)} %wv.1, bf16[4,256]{1,0:T(4,128)(2,1)} %cq.1, ...), custom_call_target="tpu_custom_call" | custom-call | tf_op jit(solution)/shard_map/gla/pallas_call | solution.py:626
  52.1 0.9 %write_out.1 = (bf16[64,2048]{1,0:T(8,128)(2,1)}, f32[256,512]{1,0:T(8,128)}, bf16[1,1,3,1024]{3,2,1,0:T(4,128)(2,1)}) custom-call(bf16[64,2048]{1,0:T(8,128)(2,1)S(1)} %get-tuple-element.9.mixed, f32[256,512]{1,0:T(8,128)S(1)} %get-tuple-element.10.states, bf16[1,1,3,1024]{3,2,1,0:T(4,128)(2,1)S(1)} %get-tuple-element.11.edges), custom_call_target="tpu_custom_call" | custom-call | tf_op jit(solution)/shard_map/write_out/pallas_call | solution.py:726

commit v7 on v6

--- a/solution.py
+++ b/solution.py
@@ -542,12 +542,11 @@
         rs_s[c] = project(gated, c).astype(BF16)
         (to_right if c < 2 else to_left)(c, relay.at[c], relay_recv.at[c]).start()
     gated_r = heads(right)
-    gated_l = heads(left)
-    for i in range(2):
-        c = 2 + i
+    for c in (2, 3):
         rs_s[4 + c] = project(gated_r, c).astype(BF16)
         to_right(4 + c, fin.at[c, 0], f_recv.at[c]).start()
-        c = i
+    gated_l = heads(left)
+    for c in (0, 1):
         rs_s[4 + c] = project(gated_l, c).astype(BF16)
         to_left(4 + c, fin.at[c, 1], f_recv.at[c]).start()
     for i in range(2):

time: 53.1 us -> 53.1 us (level)
  no operation moved by 1% of the time
where the time goes in v7:
time: 53.1 us; the launch traced here: 53 us
  Pallas kernels  52.3 us (98%)
  between operations  0.64 us (1%)
    pallas_call x1, Pallas kernels, shards(): pl.pallas_call(kernel, out_shape=(pltpu.VMEM((ROWS, D), BF16), pltpu.VMEM...  51.4 us

profile of v7, /device:TPU:1, one launch (start us, length us, event | category | flops | bytes accessed | tf_op | source)
XLA Modules:
  0.0 53.0 jit_solution(12128500932459915691)
XLA Ops:
  0.6 51.4 %gla.1 = (bf16[64,2048]{1,0:T(8,128)(2,1)S(1)}, f32[256,512]{1,0:T(8,128)S(1)}, bf16[1,1,3,1024]{3,2,1,0:T(4,128)(2,1)S(1)}) custom-call(bf16[64,2048]{1,0:T(8,128)(2,1)} %tokens.1, s32[33]{0:T(128)} %lengths.1, bf16[2048,256]{1,0:T(8,128)(2,1)} %wq.1, bf16[2048,256]{1,0:T(8,128)(2,1)} %wk.1, bf16[2048,512]{1,0:T(8,128)(2,1)} %wv.1, bf16[4,256]{1,0:T(4,128)(2,1)} %cq.1, ...), custom_call_target="tpu_custom_call" | custom-call | tf_op jit(solution)/shard_map/gla/pallas_call | solution.py:625
  52.1 0.9 %write_out.1 = (bf16[64,2048]{1,0:T(8,128)(2,1)}, f32[256,512]{1,0:T(8,128)}, bf16[1,1,3,1024]{3,2,1,0:T(4,128)(2,1)}) custom-call(bf16[64,2048]{1,0:T(8,128)(2,1)S(1)} %get-tuple-element.9.mixed, f32[256,512]{1,0:T(8,128)S(1)} %get-tuple-element.10.states, bf16[1,1,3,1024]{3,2,1,0:T(4,128)(2,1)S(1)} %get-tuple-element.11.edges), custom_call_target="tpu_custom_call" | custom-call | tf_op jit(solution)/shard_map/write_out/pallas_call | solution.py:725
